TPU v7x, 512 devices: a whole 4x8x8 slice. The times are simulated.
512 devices in a mesh: ctx: 32 (over x, z), heads: 8 (over y), dp: 2 (over core).
Axes of the slice: x: 4, y: 8, z: 8, core: 2. Of those that a mesh axis runs over, the one named last changes fastest.
Arguments:
- queries: bfloat16 [2, 8192, 8192], P('dp', 'ctx', 'heads'), may hold values from -6 to 6
- keys: bfloat16 [2, 8192, 8192], P('dp', 'ctx', 'heads'), may hold values from -6 to 6
- values: bfloat16 [2, 8192, 8192], P('dp', 'ctx', 'heads'), may hold values from -76 to 76, as said below
- gain: float32 [8192], P('heads'), may hold values from 0.1 to 1.9
- grad_out: bfloat16 [2, 8192, 8192], P('dp', 'ctx', 'heads'), may hold values from -6 to 6
Outputs:
- output: bfloat16 [2, 8192, 8192], P('dp', 'ctx', 'heads')
- grad_queries: bfloat16 [2, 8192, 8192], P('dp', 'ctx', 'heads')
- grad_keys: bfloat16 [2, 8192, 8192], P('dp', 'ctx', 'heads')
- grad_values: bfloat16 [2, 8192, 8192], P('dp', 'ctx', 'heads')
- grad_gain: float32 [8192], P('heads')
Inputs may be any that keep to these rules, and one draw needn't show every extreme that they name: The values' columns are scaled so that their size grows about threefold from the first head to the last, with further random scales per column and per token.
All inputs are finite; a program needn't handle non-finite values.
Results may differ from a plain program's by a relative error of at most 0.0012.
Values sent between devices are 32-bit elements; how exact they have to be, the bound alone decides.
No kernel may reach another device: no remote copies, remote signals or barrier semaphores. Data moves between devices by JAX's collectives and lax.ppermute only.
A program may use at most 128 MiB of HBM per device.

v0:
```python
import math

import jax
import jax.numpy as jnp
from jax import lax
from jax.sharding import PartitionSpec as P

DH = 128


epsilon = 1e-05


def carried_in(part, axis, combine, identity, reverse):
    count = lax.axis_size(axis)
    place = lax.axis_index(axis)
    ahead = count - 1 - place if reverse else place
    gathered = lax.all_gather(part, axis)
    state = jnp.zeros_like(part) + jnp.asarray(identity, part.dtype)

    def one(hop, state):
        source = count - 1 - hop if reverse else hop
        return combine(state, lax.dynamic_index_in_dim(gathered, source, 0, False))

    return lax.fori_loop(0, ahead, one, state)


def to_blocks(array, rows):
    tokens = array.shape[1]
    per_head = array.shape[2] // DH
    return array[0].reshape(tokens // rows, rows, per_head, DH).transpose(0, 2, 1, 3)


def from_blocks(array):
    count, per_head, rows, width = array.shape
    return array.transpose(0, 2, 1, 3).reshape(1, count * rows, per_head * width)


def run_forward(block_q, block_k, block_v, start, mask, scale):

    def advance(state, item):
        q_block, k_block, v_block = item
        scaled = q_block.astype(jnp.float32) * scale
        k_full = k_block.astype(jnp.float32)
        v_full = v_block.astype(jnp.float32)
        scores = jnp.einsum("hid,hjd->hij", scaled, k_full, precision=lax.Precision.HIGHEST) * mask
        out = jnp.einsum("hij,hjd->hid", scores, v_full, precision=lax.Precision.HIGHEST)
        out = out + jnp.einsum("hid,hde->hie", scaled, state, precision=lax.Precision.HIGHEST)
        after = state + jnp.einsum("hid,hie->hde", k_full, v_full, precision=lax.Precision.HIGHEST)
        return (after, (out, state))

    return lax.scan(advance, start, (block_q, block_k, block_v))


def run_backward(block_q, block_k, block_v, d_attn, starts, grad_start, mask, scale):

    def retreat(grad_state, item):
        q_block, k_block, v_block, d_block, state = item
        scaled = q_block.astype(jnp.float32) * scale
        k_full = k_block.astype(jnp.float32)
        v_full = v_block.astype(jnp.float32)
        scores = jnp.einsum("hid,hjd->hij", scaled, k_full, precision=lax.Precision.HIGHEST) * mask
        d_scores = (
            jnp.einsum("hie,hje->hij", d_block, v_full, precision=lax.Precision.HIGHEST) * mask
        )
        d_query = jnp.einsum("hij,hjd->hid", d_scores, k_full, precision=lax.Precision.HIGHEST)
        d_query = (
            d_query + jnp.einsum("hie,hde->hid", d_block, state, precision=lax.Precision.HIGHEST)
        ) * scale
        d_key = jnp.einsum("hij,hid->hjd", d_scores, scaled, precision=lax.Precision.HIGHEST)
        d_key = d_key + jnp.einsum(
            "hje,hde->hjd", v_full, grad_state, precision=lax.Precision.HIGHEST
        )
        d_value = jnp.einsum("hij,hie->hje", scores, d_block, precision=lax.Precision.HIGHEST)
        d_value = d_value + jnp.einsum(
            "hjd,hde->hje", k_full, grad_state, precision=lax.Precision.HIGHEST
        )
        after = grad_state + jnp.einsum(
            "hid,hie->hde", scaled, d_block, precision=lax.Precision.HIGHEST
        )
        return (after, (d_query, d_key, d_value))

    return lax.scan(retreat, grad_start, (block_q, block_k, block_v, d_attn, starts), reverse=True)


def add_states(earlier, later):
    return earlier + later


def prefix_states(local):
    return carried_in(local, "ctx", add_states, jnp.zeros_like(local), False)


def suffix_states(local):
    return carried_in(local, "ctx", add_states, jnp.zeros_like(local), True)


def body(queries, keys, values, gain, grad_out):
    tokens = queries.shape[1]
    rows = min(512, tokens)
    scale = DH ** (-0.5)
    block_q = to_blocks(queries, rows)
    block_k = to_blocks(keys, rows)
    block_v = to_blocks(values, rows)
    per_head = block_q.shape[1]
    mask = jnp.tril(jnp.ones((rows, rows), jnp.float32))
    local = jnp.einsum("nhjd,nhje->hde", block_k, block_v, preferred_element_type=jnp.float32)
    prefix = prefix_states(local)
    _, (attn, starts) = run_forward(block_q, block_k, block_v, prefix, mask, scale)
    columns = lax.axis_size("heads") * per_head * DH
    gains = gain.reshape(1, per_head, 1, DH)
    d_out = to_blocks(grad_out, rows).astype(jnp.float32)
    weighted = gains * d_out
    squares, inner = lax.psum(
        (jnp.sum(attn * attn, axis=(1, 3)), jnp.sum(weighted * attn, axis=(1, 3))), "heads"
    )
    root = jnp.sqrt(squares / columns + epsilon)[:, None, :, None]
    inner = inner[:, None, :, None]
    unit_attn = attn / root
    output = from_blocks(gains * unit_attn).astype(jnp.bfloat16)
    d_attn = weighted / root - attn * inner / (columns * root**3)
    partial_gain = jnp.sum(d_out * unit_attn, axis=(0, 2)).reshape(per_head * DH)
    total_rows = lax.axis_size("dp") * lax.axis_size("ctx") * tokens
    grad_gain = lax.psum(partial_gain, ("ctx", "dp")) / math.sqrt(total_rows)
    scaled_all = block_q.astype(jnp.float32) * scale
    local_grad = jnp.einsum("nhid,nhie->hde", scaled_all, d_attn, precision=lax.Precision.HIGHEST)
    suffix = suffix_states(local_grad)
    _, (d_query, d_key, d_value) = run_backward(
        block_q, block_k, block_v, d_attn, starts, suffix, mask, scale
    )
    return (
        output,
        from_blocks(d_query).astype(jnp.bfloat16),
        from_blocks(d_key).astype(jnp.bfloat16),
        from_blocks(d_value).astype(jnp.bfloat16),
        grad_gain,
    )


def solution(mesh):
    placed = (
        P("dp", "ctx", "heads"),
        P("dp", "ctx", "heads"),
        P("dp", "ctx", "heads"),
        P("heads"),
        P("dp", "ctx", "heads"),
    )
    return jax.shard_map(
        body,
        mesh=mesh,
        in_specs=placed,
        out_specs=(
            P("dp", "ctx", "heads"),
            P("dp", "ctx", "heads"),
            P("dp", "ctx", "heads"),
            P("dp", "ctx", "heads"),
            P("heads"),
        ),
        check_vma=False,
    )
```

profile of v0, /device:TPU:1, one launch (start us, length us, event | category | flops | bytes accessed | tf_op | source)
XLA Modules:
  0.0 435.9 jit_solution(8909920843852030330)
XLA Ops:
  7.2 1.2 copy.66
  8.5 0.8 copy-done.5
  9.3 1.1 fusion.45
  10.5 0.9 copy.65
  11.4 1.2 copy.36
  12.7 0.3 copy.56
  13.1 1.9 bitcast_bitcast_fusion.1
  15.0 2.4 fusion.46
  17.3 146.3 %all-gather.5.cloned.1.call-done = f32[256,128,128]{2,1,0:T(8,128)} async-done(((f32[8,128,128]{2,1,0:T(8,128)}), f32[256,128,128]{2,1,0:T(8,128)}) %all-gather.5.cloned.1.call-update) | async-done | bytes 16777232 | tf_op jit(solution)/shard_map/all_gather | solution.py:18
  163.7 1.1 fusion.57
  164.8 0.5 copy-done
  165.4 1.5 multiply_reduce_fusion
  166.9 13.4 %psum.21 = f32[1,256]{1,0:T(1,128)S(1)} all-reduce(f32[1,256]{1,0:T(1,128)S(1)} %bitcast.153), channel_id=1, replica_groups=mesh['ctx'=32,'heads'=8,'dp'=2] {'heads'}, use_global_device_ids=true, to_apply=%region_3.4 | all-reduce | flops 256 | bytes 2048 | tf_op jit(solution)/shard_map/psum | solution.py:114
  180.3 1.6 fusion.32
  182.0 11.5 %psum.22 = f32[256]{0:T(256)S(1)} all-reduce(f32[256]{0:T(256)S(1)} %get-tuple-element.154), channel_id=1, replica_groups=mesh['ctx'=32,'heads'=8,'dp'=2] {'heads'}, use_global_device_ids=true, to_apply=%region_5.6 | all-reduce | flops 256 | bytes 2048 | tf_op jit(solution)/shard_map/psum | solution.py:114
  193.5 1.8 bitcast_subtract_fusion
  195.2 1.9 fusion.34
  197.2 2.2 multiply_convert_fusion
  199.4 2.0 copy.42
  201.4 1.1 fusion.36
  202.5 1.0 fusion.38
  203.6 2.2 fusion.23
  205.8 2.0 copy.43
  207.9 167.5 %psum.23 = f32[1024]{0:T(1024)S(1)} all-reduce(f32[1024]{0:T(1024)S(1)} %bitcast.152), channel_id=1, replica_groups=mesh['ctx'=32,'heads'=8,'dp'=2] {'ctx','dp'}, use_global_device_ids=true, to_apply=%region_9.10 | all-reduce | flops 1024 | bytes 8192 | tf_op jit(solution)/shard_map/psum | solution.py:124
  375.3 0.6 broadcast_multiply_fusion
  375.9 5.2 %all-gather.7.cloned.1.call-done = f32[256,128,128]{2,1,0:T(8,128)} async-done(((f32[8,128,128]{2,1,0:T(8,128)}), f32[256,128,128]{2,1,0:T(8,128)}) %all-gather.7.cloned.1.call-update) | async-done | bytes 16777232 | tf_op jit(solution)/shard_map/all_gather | solution.py:18
  381.2 37.1 %while.7 = (s32[]{:T(128)}, f32[8,128,128]{2,1,0:T(8,128)S(1)}, s32[]{:T(128)}, f32[32,8,128,128]{3,2,1,0:T(8,128)}, s32[]{:T(128)}, /*index=5*/s32[]{:T(128)}, s32[]{:T(128)}, s32[]{:T(128)}) while((s32[]{:T(128)}, f32[8,128,128]{2,1,0:T(8,128)S(1)}, s32[]{:T(128)}, f32[32,8,128,128]{3,2,1,0:T(8,128)}, s32[]{:T(128)}, /*index=5*/s32[]{:T(128)}, ...), condition=%wide.region_7.8_spmd, body=%wide.region_6.7_spmd.sunk | while | flops 131078 | bytes 1573007 | solution.py:25
  381.2 1.2 bitcast_add_fusion.5
  382.4 1.2 bitcast_add_fusion.5
  383.6 1.2 bitcast_add_fusion.5
  384.8 1.2 bitcast_add_fusion.5
  386.0 1.2 bitcast_add_fusion.5
  387.2 1.2 bitcast_add_fusion.5
  388.4 1.2 bitcast_add_fusion.5
  389.6 1.2 bitcast_add_fusion.5
  390.7 1.2 bitcast_add_fusion.5
  391.9 1.2 bitcast_add_fusion.5
  393.1 1.2 bitcast_add_fusion.5
  394.3 1.2 bitcast_add_fusion.5
  395.5 1.2 bitcast_add_fusion.5
  396.7 1.2 bitcast_add_fusion.5
  397.9 1.2 bitcast_add_fusion.5
  399.1 1.2 bitcast_add_fusion.5
  400.3 1.2 bitcast_add_fusion.5
  401.5 1.2 bitcast_add_fusion.5
  402.7 1.2 bitcast_add_fusion.5
  403.9 1.2 bitcast_add_fusion.5
  405.1 1.2 bitcast_add_fusion.5
  406.2 1.2 bitcast_add_fusion.5
  407.4 1.2 bitcast_add_fusion.5
  408.6 1.2 bitcast_add_fusion.5
  409.8 1.2 bitcast_add_fusion.5
  411.0 1.2 bitcast_add_fusion.5
  412.2 1.2 bitcast_add_fusion.5
  413.4 1.2 bitcast_add_fusion.5
  414.6 1.2 bitcast_add_fusion.5
  415.8 1.2 bitcast_add_fusion.5
  417.0 1.2 bitcast_add_fusion.5
  418.4 1.6 convolution_bitcast_fusion.1
  419.9 0.6 convolution_bitcast_fusion
  420.6 2.3 fusion.29
  422.9 2.0 copy.45
  425.0 3.1 fusion.26
  428.0 1.0 copy.44
  (38 shorter events, 0.5 us)
Async XLA Ops:
  7.2 2.1 copy-start.4
  7.2 156.5 %all-gather.5.cloned.1.call-start = ((), (), s32[]{:S(2)}) async-start(), calls=%async_computation | async-start | bytes 17301504 | tf_op jit(solution)/shard_map/all_gather | solution.py:18
  8.4 3.0 copy-start.11
  8.5 0.8 copy-start.5
  9.3 3.3 copy-start.12
  10.4 370.7 %all-gather.7.cloned.1.call-start = ((), (), s32[]{:S(2)}) async-start(), calls=%async_computation.1 | async-start | bytes 17301504 | tf_op jit(solution)/shard_map/all_gather | solution.py:18
  12.7 2.3 copy-start.7
  163.7 1.6 copy-start
  163.7 1.7 copy-start.10
  165.4 14.9 %copy-start.13 = (f32[1024]{0:T(1024)S(1)}, f32[1024]{0:T(1024)}, u32[]{:S(2)}) copy-start(f32[1024]{0:T(1024)} %param.12) | copy-start | bytes 12292
  166.9 15.0 %copy-start.3 = (f32[8,256,128]{1,2,0:T(8,128)}, f32[8,256,128]{1,2,0:T(8,128)S(1)}, u32[]{:S(2)}) copy-start(f32[8,256,128]{1,2,0:T(8,128)S(1)} %get-tuple-element.172) | copy-start | bytes 3145732
  202.5 1.1 copy-start.6
  203.6 2.3 copy-start.2
  418.3 1.6 copy-start.8
  418.3 2.2 copy-start.1
  420.6 4.4 %copy-start.9 = (f32[8,256,128]{1,2,0:T(8,128)S(1)}, f32[8,256,128]{1,2,0:T(8,128)}, u32[]{:S(2)}) copy-start(f32[8,256,128]{1,2,0:T(8,128)} %convolution_bitcast_fusion.1) | copy-start | bytes 3145732
Sparse Core Ops, SparseCore 0:
  11.8 151.8 all-gather.4
  197.3 183.8 all-gather.6
where the time goes:
time: 438 us; the launch traced here: 436 us
  blocking collectives  192 us (44%)
  waiting for transfers between devices  152 us (35%)
  other arithmetic  42.6 us (10%)
  matrix products  20 us (5%)
  between operations  14.3 us (3%)
  local copies, waits for them, and re-layouts  14.1 us (3%)
    psum x1, blocking collectives, body(): grad_gain = lax.psum(partial_gain, ('ctx', 'dp')) / math.sqrt(total_rows)  167 us
    all_gather x2, waiting for transfers between devices, carried_in(): gathered = lax.all_gather(part, axis)  152 us
    add x31, other arithmetic, add_states(): return earlier + later  36.3 us
    psum x2, blocking collectives, body(): lax.psum((jnp.sum(attn * attn, axis=(1, 3)), jnp.sum(weighted * attn, axi...  24.9 us
    unnamed x34, local copies, waits for them, and re-layouts  10.6 us
  transfers between devices with their start and end apart: 2, of which 2 were waited for; matrix products, arithmetic and copies ran while one was open for 4% of the time, Pallas kernels for 0%

commit v1 on v0

v1 whole, which is shorter than its diff:
```python
import functools
import math

import jax
import jax.numpy as jnp
from jax import lax
from jax.experimental import pallas as pl
from jax.experimental.pallas import tpu as pltpu
from jax.sharding import PartitionSpec as P

DH = 128
epsilon = 1e-05
STEP = 2
F32 = jnp.float32
BF16 = jnp.bfloat16


def halves(x):
    upper = x.astype(BF16)
    return upper, (x - upper.astype(F32)).astype(BF16)


def dot(a, b, ca=1, cb=0):
    return lax.dot_general(a, b, (((ca,), (cb,)), ((), ())), preferred_element_type=F32)


def exact_dot(a, b, ca, cb):
    return lax.dot_general(
        a, b, (((ca,), (cb,)), ((), ())), preferred_element_type=F32, precision=lax.Precision.HIGHEST
    )


def columns(head):
    return slice(head * DH, (head + 1) * DH)


def causal(x):
    row = lax.broadcasted_iota(jnp.int32, x.shape, 0)
    column = lax.broadcasted_iota(jnp.int32, x.shape, 1)
    return jnp.where(row >= column, x, 0.0)


def call(kernel, name, grid, ins, outs, flops, arrays):
    moved = sum(a.size * a.dtype.itemsize for a in arrays)
    moved += sum(math.prod(shape) * jnp.dtype(kind).itemsize for _, _, shape, kind in outs)
    return pl.pallas_call(
        kernel,
        name=name,
        grid=grid,
        in_specs=[pl.BlockSpec(block, index) for block, index in ins],
        out_specs=[pl.BlockSpec(block, index) for block, index, _, _ in outs],
        out_shape=[jax.ShapeDtypeStruct(shape, kind) for _, _, shape, kind in outs],
        cost_estimate=pl.CostEstimate(flops=flops, bytes_accessed=moved, transcendentals=0),
        compiler_params=pltpu.CompilerParams(vmem_limit_bytes=48 * 1024 * 1024),
    )(*arrays)


def states_kernel(k_ref, v_ref, state_ref):
    for i in range(STEP):
        at = columns(i)
        state_ref[at, :] = dot(k_ref[:, at], v_ref[:, at], 0, 0)


def inner_kernel(q_ref, k_ref, v_ref, out_ref):
    for i in range(STEP):
        at = columns(i)
        scores = causal(dot(q_ref[:, at], k_ref[:, at], 1, 1))
        upper, lower = halves(scores)
        v = v_ref[:, at]
        out_ref[:, at] = dot(upper, v) + dot(lower, v)


def scan_kernel(reverse, part_ref, out_ref):
    count = part_ref.shape[0]
    total = jnp.zeros(out_ref.shape[1:], F32)
    for i in range(count):
        place = count - 1 - i if reverse else i
        out_ref[place] = total
        total = total + part_ref[place]


def suffix_kernel(rows, part_ref, out_ref, gain_ref):
    count = part_ref.shape[0]
    total = jnp.zeros(out_ref.shape[1:], F32)
    gain = jnp.zeros(gain_ref.shape, F32)
    for i in range(count):
        place = count - 1 - i
        out_ref[place] = total
        total = total + part_ref[place, :rows]
        gain = gain + part_ref[place, rows:]
    gain_ref[...] = gain


def attend_kernel(steps, scale, q_ref, within_ref, state_ref, gain_ref, dy_ref, attn_ref, sums_ref, square_sum, inner_sum):
    step = pl.program_id(0)
    squares = jnp.zeros(square_sum.shape, F32)
    inner = jnp.zeros(inner_sum.shape, F32)
    for i in range(STEP):
        at = columns(i)
        q = q_ref[:, at]
        upper, lower = halves(state_ref[at, :])
        attn = scale * (
            within_ref[:, at]
            + dot(jnp.concatenate([q, q], 1), jnp.concatenate([upper, lower], 0))
        )
        attn_ref[:, at] = attn
        squares += attn * attn
        inner += (gain_ref[:, at] * dy_ref[:, at].astype(F32)) * attn

    @pl.when(step == 0)
    def _():
        square_sum[...] = squares
        inner_sum[...] = inner

    @pl.when(step > 0)
    def _():
        square_sum[...] += squares
        inner_sum[...] += inner

    @pl.when(step == steps - 1)
    def _():
        row = lax.broadcasted_iota(jnp.int32, (8, DH), 0)
        sums = exact_dot(jnp.where(row == 0, 1.0, 0.0), square_sum[...], 1, 1)
        sums += exact_dot(jnp.where(row == 1, 1.0, 0.0), inner_sum[...], 1, 1)
        for i in range(sums_ref.shape[0]):
            sums_ref[i] = sums


def token_factors(sums, width):
    row = lax.broadcasted_iota(jnp.int32, (sums.shape[0], DH), 0) % 8
    squares = exact_dot(sums, jnp.where(row == 0, 1.0, 0.0), 0, 0)
    inner = exact_dot(sums, jnp.where(row == 1, 1.0, 0.0), 0, 0)
    inverse = 1.0 / jnp.sqrt(squares / width + epsilon)
    return inverse, inner * (inverse * inverse * inverse) / width


def grad_state_kernel(width, sums_ref, q_ref, attn_ref, gain_ref, dy_ref, state_ref, factor_ref):
    inverse, other = token_factors(sums_ref[...], width)
    factor_ref[0] = inverse
    factor_ref[1] = other
    heads = q_ref.shape[1] // DH
    per_head = state_ref.shape[0] // heads
    rows = DH // per_head
    weights = []
    for i in range(heads):
        at = columns(i)
        dy = dy_ref[:, at].astype(F32)
        attn = attn_ref[:, at]
        weights.append(jnp.sum(dy * (attn * inverse), axis=0, keepdims=True))
        d_attn = (gain_ref[:, at] * dy) * inverse - attn * other
        upper, lower = halves(d_attn)
        q = q_ref[:, at]
        state = dot(q, upper, 0, 0) + dot(q, lower, 0, 0)
        state_ref[i * per_head : (i + 1) * per_head, :rows, :] = state.reshape(per_head, rows, DH)
    weights = jnp.concatenate(weights, 0)
    for i in range(state_ref.shape[0]):
        state_ref[i, rows:, :] = weights


def backward_kernel(scale, q_ref, k_ref, v_ref, dy_ref, gain_ref, attn_ref, state_ref, factor_ref, out_ref, dq_ref, dk_ref, dv_ref):
    inverse = factor_ref[0]
    other = factor_ref[1]
    for i in range(STEP):
        at = columns(i)
        q, k, v = q_ref[:, at], k_ref[:, at], v_ref[:, at]
        gain = gain_ref[:, at]
        attn = attn_ref[:, at]
        unit = attn * inverse
        out_ref[:, at] = (gain * unit).astype(out_ref.dtype)
        d_attn = (gain * dy_ref[:, at].astype(F32)) * inverse - attn * other
        d_upper, d_lower = halves(d_attn)
        scores = causal(dot(q, k, 1, 1))
        s_upper, s_lower = halves(scores)
        d_scores = causal(
            dot(jnp.concatenate([d_upper, d_lower], 1), jnp.concatenate([v, v], 1), 1, 1)
        )
        ds_upper, ds_lower = halves(d_scores)
        p_upper, p_lower = halves(state_ref[at, :])
        dq = dot(ds_upper, k) + dot(ds_lower, k)
        dq += dot(jnp.concatenate([d_upper, d_lower], 1), jnp.concatenate([p_upper, p_upper], 1), 1, 1)
        dq += dot(d_upper, p_lower, 1, 1)
        dq_ref[:, at] = (scale * dq).astype(dq_ref.dtype)
        dk_ref[:, at] = dot(ds_upper, q, 0, 0) + dot(ds_lower, q, 0, 0)
        dv_ref[:, at] = dot(s_upper, d_upper, 0, 0) + dot(s_upper, d_lower, 0, 0) + dot(s_lower, d_upper, 0, 0)


def last_kernel(scale, k_ref, v_ref, state_ref, dk_in, dv_in, dk_ref, dv_ref):
    for i in range(STEP):
        at = columns(i)
        k, v = k_ref[:, at], v_ref[:, at]
        upper, lower = halves(state_ref[at, :])
        dk = dk_in[:, at] + dot(jnp.concatenate([v, v], 1), jnp.concatenate([upper, lower], 1), 1, 1)
        dv = dv_in[:, at] + dot(jnp.concatenate([k, k], 1), jnp.concatenate([upper, lower], 0))
        dk_ref[:, at] = (scale * dk).astype(dk_ref.dtype)
        dv_ref[:, at] = (scale * dv).astype(dv_ref.dtype)


def body(queries, keys, values, gain, grad_out):
    _, tokens, wide = queries.shape
    q, k, v, dy = (a.reshape(tokens, wide) for a in (queries, keys, values, grad_out))
    gain = gain.reshape(1, wide)
    heads = wide // DH
    ctx, shards = lax.axis_size("ctx"), lax.axis_size("heads")
    width = float(shards * wide)
    scale = DH ** (-0.5)
    steps = heads // STEP
    rows = wide // ctx
    cols = STEP * DH
    per = 2 * tokens * DH * DH * heads

    tok = ((tokens, cols), lambda i: (0, i))
    state = ((cols, DH), lambda i: (i, 0))
    vec = ((1, cols), lambda i: (0, i))
    all_tok = (tokens, wide)

    def whole(*shape):
        return (shape, lambda i: (0,) * len(shape))

    (local,) = call(
        states_kernel, "key_value_states", (steps,), [tok, tok], [(*state, (wide, DH), F32)], per, [k, v]
    )
    parts = lax.all_to_all(local, "ctx", 0, 0, tiled=True)
    (within,) = call(
        inner_kernel, "within_block", (steps,), [tok] * 3, [(*tok, all_tok, F32)], 6 * per, [q, k, v]
    )
    (before,) = call(
        functools.partial(scan_kernel, False),
        "prefix",
        (1,),
        [whole(ctx, rows, DH)],
        [(*whole(ctx, rows, DH), (ctx, rows, DH), F32)],
        wide * DH,
        [parts.reshape(ctx, rows, DH)],
    )
    prefix = lax.all_to_all(before.reshape(wide, DH), "ctx", 0, 0, tiled=True)

    moved = sum(a.size * a.dtype.itemsize for a in (q, within, prefix, dy)) + within.size * 4
    attn, sums = pl.pallas_call(
        functools.partial(attend_kernel, steps, scale),
        name="attend",
        grid=(steps,),
        in_specs=[pl.BlockSpec(*s) for s in (tok, tok, state, vec, tok)],
        out_specs=[pl.BlockSpec(*tok), pl.BlockSpec(*whole(shards, 8, tokens))],
        out_shape=[
            jax.ShapeDtypeStruct(all_tok, F32),
            jax.ShapeDtypeStruct((shards, 8, tokens), F32),
        ],
        scratch_shapes=[pltpu.VMEM((tokens, DH), F32)] * 2,
        cost_estimate=pl.CostEstimate(flops=2 * per, bytes_accessed=moved, transcendentals=0),
        compiler_params=pltpu.CompilerParams(vmem_limit_bytes=48 * 1024 * 1024),
    )(q, within, prefix, gain, dy)
    sums = lax.all_to_all(sums, "heads", 0, 0, tiled=True).reshape(shards * 8, tokens)

    grad_local, factors = call(
        functools.partial(grad_state_kernel, width),
        "grad_states",
        (1,),
        [whole(shards * 8, tokens), whole(*all_tok), whole(*all_tok), whole(1, wide), whole(*all_tok)],
        [
            (*whole(ctx, rows + heads, DH), (ctx, rows + heads, DH), F32),
            (*whole(2, tokens, DH), (2, tokens, DH), F32),
        ],
        2 * per,
        [sums, q, attn, gain, dy],
    )
    grad_parts = lax.all_to_all(grad_local, "ctx", 0, 0, tiled=True)
    output, d_query, dk_part, dv_part = call(
        functools.partial(backward_kernel, scale),
        "backward_within",
        (steps,),
        [tok, tok, tok, tok, vec, tok, state, whole(2, tokens, DH)],
        [(*tok, all_tok, BF16), (*tok, all_tok, BF16), (*tok, all_tok, F32), (*tok, all_tok, F32)],
        22 * per,
        [q, k, v, dy, gain, attn, prefix, factors],
    )
    after, gain_sum = call(
        functools.partial(suffix_kernel, rows),
        "suffix",
        (1,),
        [whole(ctx, rows + heads, DH)],
        [(*whole(ctx, rows, DH), (ctx, rows, DH), F32), (*whole(heads, DH), (heads, DH), F32)],
        wide * DH,
        [grad_parts],
    )
    suffix = lax.all_to_all(after.reshape(wide, DH), "ctx", 0, 0, tiled=True)
    total_rows = lax.axis_size("dp") * ctx * tokens
    grad_gain = lax.psum(gain_sum, "dp").reshape(wide) / math.sqrt(total_rows)
    d_key, d_value = call(
        functools.partial(last_kernel, scale),
        "key_value_gradients",
        (steps,),
        [tok, tok, state, tok, tok],
        [(*tok, all_tok, BF16), (*tok, all_tok, BF16)],
        4 * per,
        [k, v, suffix, dk_part, dv_part],
    )
    return (*(a[None] for a in (output, d_query, d_key, d_value)), grad_gain)


def solution(mesh):
    placed = P("dp", "ctx", "heads")
    return jax.shard_map(
        body,
        mesh=mesh,
        in_specs=(placed, placed, placed, P("heads"), placed),
        out_specs=(placed, placed, placed, placed, P("heads")),
        check_vma=False,
    )
```

time: 438 us -> 125 us (0.29)
  the two profiles are of different devices: /device:TPU:1 before, /device:TPU:64 now
where the time goes in v1:
time: 125 us; the launch traced here: 124 us
  blocking collectives  70.4 us (56%)
  waiting for transfers between devices  17.3 us (14%)
  Pallas kernels  15.6 us (12%)
  starting transfers between devices  10.1 us (8%)
  local copies, waits for them, and re-layouts  9.57 us (8%)
    all_to_all x1, blocking collectives, body(): parts = lax.all_to_all(local, 'ctx', 0, 0, tiled=True)  30 us
    all_to_all x1, blocking collectives, body(): grad_parts = lax.all_to_all(grad_local, 'ctx', 0, 0, tiled=True)  22.7 us
    all_to_all x1, blocking collectives, body(): lax.all_to_all(sums, 'heads', 0, 0, tiled=True).reshape(shards * 8, tokens)  15.3 us
    all_to_all x1, waiting for transfers between devices, body(): prefix = lax.all_to_all(before.reshape(wide, DH), 'ctx', 0, 0, tiled=True)  14.6 us
    pallas_call x7, Pallas kernels, call(): pl.pallas_call(kernel, name=name, grid=grid, in_specs=[pl.BlockSpec(block...  13.9 us
    unnamed x32, local copies, waits for them, and re-layouts  9.57 us
    all_to_all x1, starting transfers between devices, body(): suffix = lax.all_to_all(after.reshape(wide, DH), 'ctx', 0, 0, tiled=True)  5.14 us
    all_to_all x1, starting transfers between devices, body(): prefix = lax.all_to_all(before.reshape(wide, DH), 'ctx', 0, 0, tiled=True)  4.99 us
  transfers between devices with their start and end apart: 2, of which 2 were waited for; matrix products, arithmetic and copies ran while one was open for 0% of the time, Pallas kernels for 7%

profile of v1, /device:TPU:64, one launch (start us, length us, event | category | flops | bytes accessed | tf_op | source)
XLA Modules:
  0.0 124.3 jit_solution(16446059335827793852)
XLA Ops:
  0.6 0.0 copy-start
  0.6 1.0 copy-done
  1.7 0.0 copy-start.2
  1.7 1.0 copy-done.2
  2.7 1.1 key_value_states.1
  3.8 30.0 %all_to_all.35.part_ref = f32[32,32,128]{2,1,0:T(8,128)S(1)} all-to-all(f32[32,32,128]{2,1,0:T(8,128)S(1)} %bitcast.30), channel_id=1, replica_groups=mesh['ctx'=32,'heads'=8,'dp'=2] {'ctx'}, dimensions={0} | all-to-all | bytes 1048576 | tf_op jit(solution)/shard_map/all_to_all | solution.py:222
  33.8 0.0 copy-start.4
  33.8 0.8 prefix.1
  34.7 0.0 copy-start.1
  34.7 0.0 copy-start.3
  34.7 5.0 %all-to-all-start.1 = ((f32[32,32,128]{2,1,0:T(8,128)}), f32[32,32,128]{2,1,0:T(8,128)S(1)}, u32[]{:S(2)}, u32[]{:S(2)}) async-start(f32[32,32,128]{2,1,0:T(8,128)} %prefix.1), calls=%async_computation.1 | async-start | bytes 1048576 | tf_op jit(solution)/shard_map/all_to_all | solution.py:235
  39.7 0.0 copy-done.4
  39.7 0.0 copy-done.1
  39.7 0.0 copy-done.3
  39.7 2.3 %within_block.1.within_ref = f32[256,1024]{1,0:T(8,128)S(1)} custom-call(bf16[256,1024]{1,0:T(8,128)(2,1)S(1)} %bitcast.23, bf16[256,1024]{1,0:T(8,128)(2,1)S(1)} %bitcast.16, bf16[256,1024]{1,0:T(8,128)(2,1)S(1)} %bitcast.20), custom_call_target="tpu_custom_call" | custom-call | flops 402653184 | bytes 2621440 | tf_op jit(solution)/shard_map/within_block/pallas_call | solution.py:46
  42.0 0.0 copy-start.15
  42.0 14.6 %all-to-all-done.1 = f32[32,32,128]{2,1,0:T(8,128)S(1)} async-done(((f32[32,32,128]{2,1,0:T(8,128)}), f32[32,32,128]{2,1,0:T(8,128)S(1)}, u32[]{:S(2)}, u32[]{:S(2)}) %all-to-all-start.1) | async-done | bytes 524320 | tf_op jit(solution)/shard_map/all_to_all | solution.py:235
  56.6 0.0 copy-done.15
  56.6 0.0 copy-start.5
  56.6 1.0 copy-done.5
  57.7 0.0 copy-start.6
  57.7 1.7 %attend.1 = (f32[256,1024]{1,0:T(8,128)S(1)}, f32[8,8,256]{2,1,0:T(8,128)S(1)}) custom-call(bf16[256,1024]{1,0:T(8,128)(2,1)S(1)} %bitcast.24, f32[256,1024]{1,0:T(8,128)S(1)} %within_block.1.within_ref, f32[1024,128]{1,0:T(8,128)S(1)} %bitcast.27, f32[1,1024]{1,0:T(1,128)S(1)} %bitcast.35, bf16[256,1024]{1,0:T(8,128)(2,1)S(1)} %bitcast.31), custom_call_target="tpu_custom_call" | custom-call | flops 134217728 | bytes 3670016 | tf_op jit(solution)/shard_map/attend/pallas_call | solution.py:238
  59.3 0.0 copy-start.12
  59.3 15.3 %all_to_all.36 = f32[8,8,256]{2,1,0:T(8,128)S(1)} all-to-all(f32[8,8,256]{2,1,0:T(8,128)S(1)} %get-tuple-element.18), channel_id=1, replica_groups=mesh['ctx'=32,'heads'=8,'dp'=2] {'heads'}, dimensions={0} | all-to-all | bytes 131072 | tf_op jit(solution)/shard_map/all_to_all | solution.py:252
  74.6 0.0 copy-done.6
  74.6 1.2 grad_states.1
  75.8 0.0 copy-done.12
  75.8 22.7 %all_to_all.37.part_ref = f32[32,40,128]{2,1,0:T(8,128)S(1)} all-to-all(f32[32,40,128]{2,1,0:T(8,128)S(1)} %get-tuple-element.22), channel_id=1, replica_groups=mesh['ctx'=32,'heads'=8,'dp'=2] {'ctx'}, dimensions={0} | all-to-all | bytes 1310720 | tf_op jit(solution)/shard_map/all_to_all | solution.py:266
  98.5 0.1 suffix.1
  98.6 0.0 copy-start.14
  98.6 0.8 copy-done.14
  99.4 0.0 copy-start.7
  99.4 5.1 %all-to-all-start.4 = ((f32[32,32,128]{2,1,0:T(8,128)}), f32[32,32,128]{2,1,0:T(8,128)S(1)}, u32[]{:S(2)}, u32[]{:S(2)}) async-start(f32[32,32,128]{2,1,0:T(8,128)} %copy-done.14), calls=%async_computation.4 | async-start | bytes 1048576 | tf_op jit(solution)/shard_map/all_to_all | solution.py:285
  104.5 0.0 copy-done.7
  104.5 0.0 copy-start.13
  104.5 1.2 copy-done.13
  105.8 5.9 %backward_within.1 = (bf16[256,1024]{1,0:T(8,128)(2,1)}, bf16[256,1024]{1,0:T(8,128)(2,1)}, f32[256,1024]{1,0:T(8,128)S(1)}, f32[256,1024]{1,0:T(8,128)S(1)}) custom-call(bf16[256,1024]{1,0:T(8,128)(2,1)S(1)} %bitcast.26, bf16[256,1024]{1,0:T(8,128)(2,1)S(1)} %bitcast.17, bf16[256,1024]{1,0:T(8,128)(2,1)S(1)} %bitcast.21, bf16[256,1024]{1,0:T(8,128)(2,1)S(1)} %bitcast.33, ...), custom_call_target="tpu_custom_call" | custom-call | flops 1476395008 | bytes 7081984 | tf_op jit(solution)/shard_map/backward_within/pallas_call | solution.py:46
  111.7 0.0 copy-start.8
  111.7 1.0 copy-done.8
  112.7 0.0 copy-start.10
  112.7 1.0 copy-done.10
  113.6 2.4 %psum.7 = f32[8,128]{1,0:T(8,128)S(1)} all-reduce(f32[8,128]{1,0:T(8,128)S(1)} %get-tuple-element.28), channel_id=1, replica_groups=mesh['ctx'=32,'heads'=8,'dp'=2] {'dp'}, use_global_device_ids=true, to_apply=%region_0.0 | all-reduce | flops 1024 | bytes 8192 | tf_op jit(solution)/shard_map/psum | solution.py:287
  116.1 0.6 multiply_bitcast_fusion
  116.7 2.7 %all-to-all-done.4 = f32[32,32,128]{2,1,0:T(8,128)S(1)} async-done(((f32[32,32,128]{2,1,0:T(8,128)}), f32[32,32,128]{2,1,0:T(8,128)S(1)}, u32[]{:S(2)}, u32[]{:S(2)}) %all-to-all-start.4) | async-done | bytes 524320 | tf_op jit(solution)/shard_map/all_to_all | solution.py:285
  119.4 0.0 copy-start.9
  119.4 1.2 copy-done.9
  120.6 0.0 copy-start.11
  120.6 1.2 copy-done.11
  121.8 2.5 %key_value_gradients.1 = (bf16[256,1024]{1,0:T(8,128)(2,1)}, bf16[256,1024]{1,0:T(8,128)(2,1)}) custom-call(bf16[256,1024]{1,0:T(8,128)(2,1)S(1)} %bitcast.18, bf16[256,1024]{1,0:T(8,128)(2,1)S(1)} %bitcast.22, f32[1024,128]{1,0:T(8,128)S(1)} %bitcast.29, f32[256,1024]{1,0:T(8,128)S(1)} %copy-done.9, f32[256,1024]{1,0:T(8,128)S(1)} %copy-done.11), custom_call_target="tpu_custom_call" | custom-call | flops 268435456 | bytes 4718592 | tf_op jit(solution)/shard_map/key_value_gradients/pallas_call | solution.py:46
Async XLA Ops:
  0.6 1.0 copy-start
  1.7 1.0 copy-start.2
  33.8 5.8 %copy-start.4 = (bf16[1,256,1024]{2,1,0:T(8,128)(2,1)S(1)}, bf16[1,256,1024]{2,1,0:T(8,128)(2,1)}, u32[]{:S(2)}) copy-start(bf16[1,256,1024]{2,1,0:T(8,128)(2,1)} %param.5) | copy-start | bytes 1572868
  34.7 5.0 %copy-start.1 = (bf16[1,256,1024]{2,1,0:T(8,128)(2,1)S(1)}, bf16[1,256,1024]{2,1,0:T(8,128)(2,1)}, u32[]{:S(2)}) copy-start(bf16[1,256,1024]{2,1,0:T(8,128)(2,1)} %param.6) | copy-start | bytes 1572868
  34.7 5.0 %copy-start.3 = (bf16[1,256,1024]{2,1,0:T(8,128)(2,1)S(1)}, bf16[1,256,1024]{2,1,0:T(8,128)(2,1)}, u32[]{:S(2)}) copy-start(bf16[1,256,1024]{2,1,0:T(8,128)(2,1)} %param.7) | copy-start | bytes 1572868
  34.7 21.9 %all-to-all-start.1 = ((f32[32,32,128]{2,1,0:T(8,128)}), f32[32,32,128]{2,1,0:T(8,128)S(1)}, u32[]{:S(2)}, u32[]{:S(2)}) async-start(f32[32,32,128]{2,1,0:T(8,128)} %prefix.1), calls=%async_computation.1 | async-start | bytes 1048576 | tf_op jit(solution)/shard_map/all_to_all | solution.py:235
  42.0 14.6 %copy-start.15 = (f32[1024]{0:T(1024)S(1)}, f32[1024]{0:T(1024)}, u32[]{:S(2)}) copy-start(f32[1024]{0:T(1024)} %param.8) | copy-start | bytes 12292
  56.6 1.0 copy-start.5
  57.7 17.0 %copy-start.6 = (bf16[1,256,1024]{2,1,0:T(8,128)(2,1)S(1)}, bf16[1,256,1024]{2,1,0:T(8,128)(2,1)}, u32[]{:S(2)}) copy-start(bf16[1,256,1024]{2,1,0:T(8,128)(2,1)} %param.9) | copy-start | bytes 1572868
  59.3 16.5 %copy-start.12 = (f32[256,1024]{1,0:T(8,128)}, f32[256,1024]{1,0:T(8,128)S(1)}, u32[]{:S(2)}) copy-start(f32[256,1024]{1,0:T(8,128)S(1)} %get-tuple-element.17.attn_ref) | copy-start | bytes 3145732
  98.6 0.8 copy-start.14
  99.4 5.2 %copy-start.7 = (bf16[1,256,1024]{2,1,0:T(8,128)(2,1)S(1)}, bf16[1,256,1024]{2,1,0:T(8,128)(2,1)}, u32[]{:S(2)}) copy-start(bf16[1,256,1024]{2,1,0:T(8,128)(2,1)} %param.9) | copy-start | bytes 1572868
  99.4 20.0 %all-to-all-start.4 = ((f32[32,32,128]{2,1,0:T(8,128)}), f32[32,32,128]{2,1,0:T(8,128)S(1)}, u32[]{:S(2)}, u32[]{:S(2)}) async-start(f32[32,32,128]{2,1,0:T(8,128)} %copy-done.14), calls=%async_computation.4 | async-start | bytes 1048576 | tf_op jit(solution)/shard_map/all_to_all | solution.py:285
  104.5 1.2 copy-start.13
  111.7 1.0 copy-start.8
  112.7 1.0 copy-start.10
  119.4 1.2 copy-start.9
  120.6 1.2 copy-start.11

commit v2 on v1

v2 whole, which is shorter than its diff:
```python
import functools
import math

import jax
import jax.numpy as jnp
from jax import lax
from jax.experimental import pallas as pl
from jax.experimental.pallas import tpu as pltpu
from jax.sharding import PartitionSpec as P

DH = 128
epsilon = 1e-05
F32 = jnp.float32
BF16 = jnp.bfloat16
VMEM_GRANT = 16 * 1024 * 1024
SUFFIX_OUT = "hbm"


def halves(x):
    upper = x.astype(BF16)
    return upper, (x - upper.astype(F32)).astype(BF16)


def dot(a, b, ca=1, cb=0):
    return lax.dot_general(a, b, (((ca,), (cb,)), ((), ())), preferred_element_type=F32)


def columns(head):
    return slice(head * DH, (head + 1) * DH)


def causal(x):
    row = lax.broadcasted_iota(jnp.int32, x.shape, 0)
    column = lax.broadcasted_iota(jnp.int32, x.shape, 1)
    return jnp.where(row >= column, x, 0.0)


def call(kernel, name, ins, outs, flops, scratch=(), aliases=None):
    spaces = {"vmem": pltpu.VMEM, "hbm": pltpu.HBM}
    arrays = [pltpu.with_memory_space_constraint(a, spaces[w]) if w else a for a, w in ins]
    moved = sum(a.size * a.dtype.itemsize for a, _ in ins)
    moved += sum(math.prod(shape) * jnp.dtype(kind).itemsize for shape, kind, _ in outs)

    def spec(where):
        return pl.BlockSpec(memory_space=pl.ANY if where == "hbm" else pltpu.VMEM)

    return pl.pallas_call(
        kernel,
        name=name,
        in_specs=[spec(w) for _, w in ins],
        out_specs=[spec("hbm" if w == "hbm raw" else "") for _, _, w in outs],
        out_shape=[
            spaces["hbm" if w == "hbm raw" else w](shape, kind) if w else jax.ShapeDtypeStruct(shape, kind)
            for shape, kind, w in outs
        ],
        scratch_shapes=scratch,
        input_output_aliases=aliases or {},
        cost_estimate=pl.CostEstimate(flops=flops, bytes_accessed=moved, transcendentals=0),
        compiler_params=pltpu.CompilerParams(vmem_limit_bytes=VMEM_GRANT),
    )(*arrays)


def fetch(pairs, sems):
    copies = [pltpu.make_async_copy(src, dst, sems.at[i]) for i, (src, dst) in enumerate(pairs)]
    for copy in copies:
        copy.start()
    return copies


def attend_within(q_ref, k_ref, v_ref, within_ref):
    for head in range(q_ref.shape[1] // DH):
        at = columns(head)
        upper, lower = halves(causal(dot(q_ref[:, at], k_ref[:, at], 1, 1)))
        v = v_ref[:, at]
        within_ref[:, at] = dot(upper, v) + dot(lower, v)


def states_kernel(q_hbm, k_hbm, v_hbm, dy_hbm, gain_hbm, state_ref, within_ref, q_ref, dy_ref, gain_ref, k_ref, v_ref, sems):
    first = lax.axis_index("dp") == 0
    near = fetch(((k_hbm, k_ref), (v_hbm, v_ref)), sems)
    later = [
        pltpu.make_async_copy(src, dst, sems.at[2 + i])
        for i, (src, dst) in enumerate(((q_hbm, q_ref), (dy_hbm, dy_ref), (gain_hbm, gain_ref)))
    ]

    @pl.when(first)
    def _():
        for copy in later:
            copy.start()

    for copy in near:
        copy.wait()
    for head in range(k_ref.shape[1] // DH):
        at = columns(head)
        state_ref[at, :] = dot(k_ref[:, at], v_ref[:, at], 0, 0)

    @pl.when(first)
    def _():
        for copy in later:
            copy.wait()
        attend_within(q_ref, k_ref, v_ref, within_ref)


def within_kernel(q_hbm, k_hbm, v_hbm, dy_hbm, gain_hbm, *refs):
    within_ref, q_ref, dy_ref, gain_ref, k_ref, v_ref, sems = refs[4:]

    @pl.when(lax.axis_index("dp") != 0)
    def _():
        copies = fetch(
            ((q_hbm, q_ref), (k_hbm, k_ref), (v_hbm, v_ref), (dy_hbm, dy_ref), (gain_hbm, gain_ref)), sems
        )
        for copy in copies:
            copy.wait()
        attend_within(q_ref, k_ref, v_ref, within_ref)


def scan(part_ref, out_ref, out_hbm, sems, reverse):
    count, rows = part_ref.shape[0], out_ref.shape[1]
    group = count // sems.shape[0]
    total = jnp.zeros(out_ref.shape[1:], F32)
    copies = []
    for i in range(count):
        place = count - 1 - i if reverse else i
        out_ref[place] = total
        total = total + part_ref[place, :rows]
        if i % group == group - 1:
            at = pl.ds(place if reverse else place + 1 - group, group)
            copies.append(pltpu.make_async_copy(out_ref.at[at], out_hbm.at[at], sems.at[len(copies)]))
            copies[-1].start()
    return copies


def prefix_kernel(part_ref, out_hbm, out_ref, sems):
    for copy in scan(part_ref, out_ref, out_hbm, sems, False):
        copy.wait()


def suffix_kernel(gain_scale, part_ref, _, out_hbm, gain_ref, out_ref, sems):
    copies = scan(part_ref, out_ref, out_hbm, sems, True)
    rows = out_ref.shape[1]
    gain = jnp.zeros(gain_ref.shape, F32)
    for i in range(part_ref.shape[0]):
        gain = gain + part_ref[i, rows:]
    gain_ref[...] = gain_scale * gain
    for copy in copies:
        copy.wait()


def attend_kernel(scale, q_ref, within_ref, state_ref, gain_ref, dy_ref, attn_ref, sums_ref):
    tokens = q_ref.shape[0]
    squares = jnp.zeros((tokens, DH), F32)
    inner = jnp.zeros((tokens, DH), F32)
    for head in range(q_ref.shape[1] // DH):
        at = columns(head)
        q = q_ref[:, at]
        upper, lower = halves(state_ref[at, :])
        before = dot(jnp.concatenate([q, q], 1), jnp.concatenate([upper, lower], 0))
        attn = scale * (within_ref[:, at] + before)
        attn_ref[:, at] = attn
        squares += attn * attn
        inner += (gain_ref[:, at] * dy_ref[:, at].astype(F32)) * attn
    row = lax.broadcasted_iota(jnp.int32, (8, tokens), 0)
    sums = jnp.where(
        row == 0,
        jnp.sum(squares.T, axis=0, keepdims=True),
        jnp.where(row == 1, jnp.sum(inner.T, axis=0, keepdims=True), 0.0),
    )
    for i in range(sums_ref.shape[0]):
        sums_ref[i] = sums


def token_factors(sums_ref, width):
    sums = sums_ref[0]
    for i in range(1, sums_ref.shape[0]):
        sums = sums + sums_ref[i]
    inverse = 1.0 / jnp.sqrt(sums[0:1] / width + epsilon)
    other = sums[1:2] * (inverse * inverse * inverse) / width
    row = lax.broadcasted_iota(jnp.int32, sums.shape, 0)
    both = jnp.where(row == 0, inverse, other).T
    return tuple(jnp.broadcast_to(both[:, i : i + 1], (both.shape[0], DH)) for i in range(2))


def grad_state_kernel(width, sums_ref, q_ref, attn_ref, gain_ref, dy_ref, state_hbm, factor_ref, state_ref, sems):
    inverse, other = token_factors(sums_ref, width)
    factor_ref[0] = inverse
    factor_ref[1] = other
    heads = q_ref.shape[1] // DH
    per_head = state_ref.shape[0] // heads
    rows = DH // per_head
    copies = []

    def send(slices, part):
        at = (slices, part)
        copies.append(pltpu.make_async_copy(state_ref.at[at], state_hbm.at[at], sems.at[len(copies)]))
        copies[-1].start()

    weights = []
    for head in range(heads):
        at = columns(head)
        weights.append(jnp.sum(dy_ref[:, at].astype(F32) * (attn_ref[:, at] * inverse), axis=0, keepdims=True))
    weights = jnp.concatenate(weights, 0)
    for i in range(state_ref.shape[0]):
        state_ref[i, rows:, :] = weights
    send(pl.ds(0, state_ref.shape[0]), pl.ds(rows, heads))
    for head in range(heads):
        at = columns(head)
        d_attn = (gain_ref[:, at] * dy_ref[:, at].astype(F32)) * inverse - attn_ref[:, at] * other
        upper, lower = halves(d_attn)
        q = q_ref[:, at]
        state = dot(q, upper, 0, 0) + dot(q, lower, 0, 0)
        state_ref[head * per_head : (head + 1) * per_head, :rows, :] = state.reshape(per_head, rows, DH)
        if head % 2:
            send(pl.ds((head - 1) * per_head, 2 * per_head), pl.ds(0, rows))
    for copy in copies:
        copy.wait()


def backward_kernel(scale, q_hbm, k_hbm, v_hbm, dy_hbm, gain_ref, attn_ref, state_ref, factor_ref, out_ref, dq_ref, dk_ref, dv_ref, k_ref, v_ref, q_ref, dy_ref, sems):
    copies = fetch(((q_hbm, q_ref), (k_hbm, k_ref), (v_hbm, v_ref), (dy_hbm, dy_ref)), sems)
    for copy in copies:
        copy.wait()
    inverse = factor_ref[0]
    other = factor_ref[1]
    for head in range(q_ref.shape[1] // DH):
        at = columns(head)
        q, k, v = q_ref[:, at], k_ref[:, at], v_ref[:, at]
        gain = gain_ref[:, at]
        attn = attn_ref[:, at]
        out_ref[:, at] = (gain * (attn * inverse)).astype(out_ref.dtype)
        d_attn = (gain * dy_ref[:, at].astype(F32)) * inverse - attn * other
        d_upper, d_lower = halves(d_attn)
        d_both = jnp.concatenate([d_upper, d_lower], 1)
        s_upper, s_lower = halves(causal(dot(q, k, 1, 1)))
        ds_upper, ds_lower = halves(causal(dot(d_both, jnp.concatenate([v, v], 1), 1, 1)))
        p_upper, p_lower = halves(state_ref[at, :])
        dq = dot(ds_upper, k) + dot(ds_lower, k)
        dq += dot(d_both, jnp.concatenate([p_upper, p_upper], 1), 1, 1)
        dq += dot(d_upper, p_lower, 1, 1)
        dq_ref[:, at] = (scale * dq).astype(dq_ref.dtype)
        dk_ref[:, at] = dot(ds_upper, q, 0, 0) + dot(ds_lower, q, 0, 0)
        dv_ref[:, at] = dot(s_upper, d_upper, 0, 0) + dot(s_upper, d_lower, 0, 0) + dot(s_lower, d_upper, 0, 0)


def return_kernel(k_hbm, v_hbm, dk_hbm, dv_hbm, gain_a, gain_b, _, k_ref, v_ref, dk_ref, dv_ref, gain_ref, sems):
    v_half = v_hbm.at[:, pl.ds(0, v_ref.shape[1])]
    copies = fetch(((k_hbm, k_ref), (v_half, v_ref), (dk_hbm, dk_ref), (dv_hbm, dv_ref)), sems)
    gain_ref[...] = gain_a[...] + gain_b[...]
    for copy in copies:
        copy.wait()


def last_kernel(scale, k_ref, v_near, v_hbm, state_ref, dk_in, dv_in, dk_hbm, dv_hbm, v_far, dk_ref, dv_ref, sems):
    wide = v_near.shape[1]
    heads = k_ref.shape[1] // DH
    half = heads // 2
    v_copy = pltpu.make_async_copy(v_hbm.at[:, pl.ds(wide, wide)], v_far, sems.at[4])
    v_copy.start()
    copies = []

    def store(src, dst, part):
        at = pl.ds(part * wide, wide)
        copies.append(pltpu.make_async_copy(src.at[:, at], dst.at[:, at], sems.at[len(copies)]))
        copies[-1].start()

    states = []
    for head in range(heads):
        at = columns(head)
        upper, lower = halves(state_ref[at, :])
        states.append((upper, lower))
        k = k_ref[:, at]
        dv = dv_in[:, at] + dot(jnp.concatenate([k, k], 1), jnp.concatenate([upper, lower], 0))
        dv_ref[:, at] = (scale * dv).astype(dv_ref.dtype)
        if head % half == half - 1:
            store(dv_ref, dv_hbm, head // half)
    for head in range(heads):
        at = columns(head)
        if head == half:
            v_copy.wait()
        v = v_near[:, at] if head < half else v_far[:, columns(head - half)]
        dk = dk_in[:, at] + dot(jnp.concatenate([v, v], 1), jnp.concatenate(states[head], 1), 1, 1)
        dk_ref[:, at] = (scale * dk).astype(dk_ref.dtype)
        if head % half == half - 1:
            store(dk_ref, dk_hbm, head // half)
    for copy in copies:
        copy.wait()


def body(queries, keys, values, gain, grad_out):
    _, tokens, wide = queries.shape
    q, k, v, dy = (a.reshape(tokens, wide) for a in (queries, keys, values, grad_out))
    gain = gain.reshape(1, wide)
    heads = wide // DH
    ctx, shards = lax.axis_size("ctx"), lax.axis_size("heads")
    width = float(shards * wide)
    scale = DH ** (-0.5)
    rows = wide // ctx
    per = 2 * tokens * DH * DH * heads
    all_tok = (tokens, wide)
    exchange = functools.partial(lax.all_to_all, axis_name="ctx", split_axis=0, concat_axis=0, tiled=True)

    inputs = [(a, "hbm") for a in (q, k, v, dy, gain)]
    near = [(all_tok, F32, "vmem"), (all_tok, BF16, "vmem"), (all_tok, BF16, "vmem"), ((1, wide), F32, "vmem")]
    inner = [pltpu.VMEM(all_tok, BF16), pltpu.VMEM(all_tok, BF16), pltpu.SemaphoreType.DMA((5,))]
    local, *held = call(states_kernel, "key_value_states", inputs, [((wide, DH), F32, "")] + near, 4 * per, inner)
    parts = exchange(local).reshape(ctx, rows, DH)
    within, q_near, dy_near, gain_near = call(
        within_kernel,
        "within_block",
        inputs + [(a, "vmem") for a in held],
        near,
        6 * per,
        inner,
        {len(inputs) + i: i for i in range(len(held))},
    )
    scan_room = [pltpu.VMEM((ctx, rows, DH), F32), pltpu.SemaphoreType.DMA((4,))]
    (before,) = call(
        prefix_kernel, "prefix", [(parts, "")], [((ctx, rows, DH), F32, "hbm raw")], wide * DH, scan_room
    )
    prefix = exchange(before.reshape(wide, DH))
    attn, sums = call(
        functools.partial(attend_kernel, scale),
        "attend",
        [(q_near, "vmem"), (within, "vmem"), (prefix, ""), (gain_near, "vmem"), (dy_near, "vmem")],
        [(all_tok, F32, "vmem"), ((shards, 8, tokens), F32, "")],
        2 * per,
    )
    sums = lax.all_to_all(sums, "heads", 0, 0, tiled=True)
    grad_local, factors = call(
        functools.partial(grad_state_kernel, width),
        "grad_states",
        [(sums, ""), (q_near, "vmem"), (attn, "vmem"), (gain_near, "vmem"), (dy_near, "vmem")],
        [((ctx, rows + heads, DH), F32, "hbm raw"), ((2, tokens, DH), F32, "vmem")],
        2 * per,
        [pltpu.VMEM((ctx, rows + heads, DH), F32), pltpu.SemaphoreType.DMA((heads // 2 + 1,))],
    )
    grad_parts = exchange(grad_local)
    output, d_query, dk_part, dv_part = call(
        functools.partial(backward_kernel, scale),
        "backward_within",
        [(q, "hbm"), (k, "hbm"), (v, "hbm"), (dy, "hbm"), (gain_near, "vmem"), (attn, "vmem"), (prefix, ""), (factors, "vmem")],
        [(all_tok, BF16, "hbm"), (all_tok, BF16, "hbm"), (all_tok, F32, "hbm"), (all_tok, F32, "hbm")],
        22 * per,
        [pltpu.VMEM(all_tok, BF16)] * 4 + [pltpu.SemaphoreType.DMA((4,))],
    )
    total_rows = lax.axis_size("dp") * ctx * tokens
    after, gain_sum = call(
        functools.partial(suffix_kernel, 1.0 / math.sqrt(total_rows)),
        "suffix",
        [(grad_parts, ""), (dv_part, "hbm")],
        [((ctx, rows, DH), F32, "hbm raw"), ((heads, DH), F32, "")],
        wide * DH,
        scan_room,
    )
    suffix = exchange(after.reshape(wide, DH))
    gain_other = lax.ppermute(gain_sum, "dp", [(i, lax.axis_size("dp") - 1 - i) for i in range(lax.axis_size("dp"))])
    k_near, v_near, dk_near, dv_near, grad_gain = call(
        return_kernel,
        "return_operands",
        [(k, "hbm"), (v, "hbm"), (dk_part, "hbm"), (dv_part, "hbm"), (gain_sum, ""), (gain_other, ""), (after, "hbm")],
        [(all_tok, BF16, "vmem"), ((tokens, wide // 2), BF16, "vmem"), (all_tok, F32, "vmem"), (all_tok, F32, "vmem"), ((heads, DH), F32, "hbm")],
        wide * DH,
        [pltpu.SemaphoreType.DMA((4,))],
    )
    d_key, d_value = call(
        functools.partial(last_kernel, scale),
        "key_value_gradients",
        [(k_near, "vmem"), (v_near, "vmem"), (v, "hbm"), (suffix, ""), (dk_near, "vmem"), (dv_near, "vmem")],
        [(all_tok, BF16, "hbm raw"), (all_tok, BF16, "hbm raw")],
        4 * per,
        [pltpu.VMEM((tokens, wide // 2), BF16)] + [pltpu.VMEM(all_tok, BF16)] * 2 + [pltpu.SemaphoreType.DMA((5,))],
    )
    return (*(a[None] for a in (output, d_query, d_key, d_value)), grad_gain.reshape(wide))


def solution(mesh):
    placed = P("dp", "ctx", "heads")
    return jax.shard_map(
        body,
        mesh=mesh,
        in_specs=(placed, placed, placed, P("heads"), placed),
        out_specs=(placed, placed, placed, placed, P("heads")),
        check_vma=False,
    )
```

time: 125 us -> 114 us (0.912)
  blocking collectives: 70.4 us -> 43.5 us
  waiting for transfers between devices: 17.3 us -> 33.6 us
  local copies, waits for them, and re-layouts: 9.57 us -> 0.01 us
  starting transfers between devices: 10.1 us -> 16.5 us
  Pallas kernels: 15.6 us -> 18.9 us
    all_to_all x3 -> x2, blocking collectives: 67.9 us -> 43.5 us  [the longest x1 28.2 us: body(): parts = exchange(local).reshape(ctx, rows, DH)]
    all_to_all x2 -> x3, waiting for transfers between devices: 17.3 us -> 32.5 us  [the longest x1 15.1 us: body(): prefix = exchange(before.reshape(wide, DH))]
    unnamed x32 -> x4, local copies, waits for them, and re-layouts: 9.57 us -> 0.01 us
    all_to_all x2 -> x3, starting transfers between devices: 10.1 us -> 14.6 us  [the longest x1 4.99 us: body(): grad_parts = exchange(grad_local)]
    pallas_call x8 -> x9, Pallas kernels: 15.6 us -> 18.9 us  [call(): pl.pallas_call(kernel, name=name, in_specs=[spec(w) for _, w in ins], out...]
    psum x1 -> x0, blocking collectives: 2.44 us -> none  [body(): grad_gain = lax.psum(gain_sum, 'dp').reshape(wide) / math.sqrt(total_rows)]
    ppermute x0 -> x1, starting transfers between devices: none -> 1.92 us  [body(): lax.ppermute(gain_sum, 'dp', [(i, lax.axis_size('dp') - 1 - i) for i in r...]
  transfers between devices with their start and end apart: 2 -> 4, of which waited for: 2 -> 4; matrix products, arithmetic and copies ran while one was open for 0% -> 0% of each run, Pallas kernels for 7% -> 8%
where the time goes in v2:
time: 114 us; the launch traced here: 113 us
  blocking collectives  43.5 us (38%)
  waiting for transfers between devices  33.6 us (29%)
  Pallas kernels  18.9 us (17%)
  starting transfers between devices  16.5 us (14%)
    all_to_all x1, blocking collectives, body(): parts = exchange(local).reshape(ctx, rows, DH)  28.2 us
    pallas_call x9, Pallas kernels, call(): pl.pallas_call(kernel, name=name, in_specs=[spec(w) for _, w in ins], out...  18.9 us
    all_to_all x1, blocking collectives, body(): sums = lax.all_to_all(sums, 'heads', 0, 0, tiled=True)  15.3 us
    all_to_all x1, waiting for transfers between devices, body(): prefix = exchange(before.reshape(wide, DH))  15.1 us
    all_to_all x1, waiting for transfers between devices, body(): grad_parts = exchange(grad_local)  8.85 us
    all_to_all x1, waiting for transfers between devices, body(): suffix = exchange(after.reshape(wide, DH))  8.47 us
    all_to_all x1, starting transfers between devices, body(): grad_parts = exchange(grad_local)  4.99 us
    all_to_all x1, starting transfers between devices, body(): prefix = exchange(before.reshape(wide, DH))  4.86 us
  transfers between devices with their start and end apart: 4, of which 4 were waited for; matrix products, arithmetic and copies ran while one was open for 0% of the time, Pallas kernels for 8%

profile of v2, /device:TPU:64, one launch (start us, length us, event | category | flops | bytes accessed | tf_op | source)
XLA Modules:
  0.0 113.3 jit_solution(13164487556141644119)
XLA Ops:
  0.6 3.4 %key_value_states.1 = (f32[1024,128]{1,0:T(8,128)S(1)}, f32[256,1024]{1,0:T(8,128)S(1)}, bf16[256,1024]{1,0:T(8,128)(2,1)S(1)}, bf16[256,1024]{1,0:T(8,128)(2,1)S(1)}, f32[1,1024]{1,0:T(1,128)S(1)}) custom-call(bf16[256,1024]{1,0:T(8,128)(2,1)} %bitcast.26, bf16[256,1024]{1,0:T(8,128)(2,1)} %bitcast.22, bf16[256,1024]{1,0:T(8,128)(2,1)} %bitcast.17, ...), custom_call_target="tpu_custom_call" | custom-call | flops 268435456 | bytes 4726784 | tf_op jit(solution)/shard_map/key_value_states/pallas_call | solution.py:47
  4.1 28.2 %all_to_all.35.part_ref = f32[32,32,128]{2,1,0:T(8,128)S(1)} all-to-all(f32[32,32,128]{2,1,0:T(8,128)S(1)} %bitcast.16), channel_id=1, replica_groups=mesh['ctx'=32,'heads'=8,'dp'=2] {'ctx'}, dimensions={0} | all-to-all | bytes 1048576 | tf_op jit(solution)/shard_map/all_to_all | solution.py:305
  32.3 0.8 prefix.1
  33.1 4.9 %all-to-all-start.1 = ((f32[32,32,128]{2,1,0:T(8,128)}), f32[32,32,128]{2,1,0:T(8,128)S(1)}, u32[]{:S(2)}, u32[]{:S(2)}) async-start(f32[32,32,128]{2,1,0:T(8,128)} %prefix.1), calls=%async_computation.1 | async-start | bytes 1048576 | tf_op jit(solution)/shard_map/all_to_all | solution.py:319
  38.0 0.1 within_block.1
  38.0 15.1 %all-to-all-done.1 = f32[32,32,128]{2,1,0:T(8,128)S(1)} async-done(((f32[32,32,128]{2,1,0:T(8,128)}), f32[32,32,128]{2,1,0:T(8,128)S(1)}, u32[]{:S(2)}, u32[]{:S(2)}) %all-to-all-start.1) | async-done | bytes 524320 | tf_op jit(solution)/shard_map/all_to_all | solution.py:319
  53.2 0.6 attend.1
  53.8 0.0 copy-start
  53.8 15.3 %all_to_all.36.sums_ref = f32[8,8,256]{2,1,0:T(8,128)S(1)} all-to-all(f32[8,8,256]{2,1,0:T(8,128)S(1)} %get-tuple-element.41), channel_id=1, replica_groups=mesh['ctx'=32,'heads'=8,'dp'=2] {'heads'}, dimensions={0} | all-to-all | bytes 131072 | tf_op jit(solution)/shard_map/all_to_all | solution.py:327
  69.1 1.6 %grad_states.1 = (f32[32,40,128]{2,1,0:T(8,128)}, f32[2,256,128]{2,1,0:T(8,128)S(1)}) custom-call(f32[8,8,256]{2,1,0:T(8,128)S(1)} %all_to_all.36.sums_ref, bf16[256,1024]{1,0:T(8,128)(2,1)S(1)} %get-tuple-element.36.q_ref, f32[256,1024]{1,0:T(8,128)S(1)} %get-tuple-element.40.attn_ref, f32[1,1024]{1,0:T(1,128)S(1)} %get-tuple-element.35.gain_ref, ...), custom_call_target="tpu_custom_call" | custom-call | flops 134217728 | bytes 3084288 | tf_op jit(solution)/shard_map/grad_states/pallas_call | solution.py:47
  70.7 0.0 copy-done
  70.7 0.0 copy-start.1
  70.7 5.0 %all-to-all-start.3 = ((f32[32,40,128]{2,1,0:T(8,128)}), f32[32,40,128]{2,1,0:T(8,128)S(1)}, u32[]{:S(2)}, u32[]{:S(2)}) async-start(f32[32,40,128]{2,1,0:T(8,128)} %get-tuple-element.47), calls=%async_computation.3 | async-start | bytes 1310720 | tf_op jit(solution)/shard_map/all_to_all | solution.py:336
  75.7 0.0 copy-done.1
  75.7 7.1 %backward_within.1 = (bf16[256,1024]{1,0:T(8,128)(2,1)}, bf16[256,1024]{1,0:T(8,128)(2,1)}, f32[256,1024]{1,0:T(8,128)}, f32[256,1024]{1,0:T(8,128)}) custom-call(bf16[256,1024]{1,0:T(8,128)(2,1)} %bitcast.28, bf16[256,1024]{1,0:T(8,128)(2,1)} %bitcast.24, bf16[256,1024]{1,0:T(8,128)(2,1)} %bitcast.19, bf16[256,1024]{1,0:T(8,128)(2,1)} %bitcast.31, ...), custom_call_target="tpu_custom_call" | custom-call | flops 1476395008 | bytes 7081984 | tf_op jit(solution)/shard_map/backward_within/pallas_call | solution.py:47
  82.9 8.8 %all-to-all-done.3.part_ref = f32[32,40,128]{2,1,0:T(8,128)S(1)} async-done(((f32[32,40,128]{2,1,0:T(8,128)}), f32[32,40,128]{2,1,0:T(8,128)S(1)}, u32[]{:S(2)}, u32[]{:S(2)}) %all-to-all-start.3) | async-done | bytes 655392 | tf_op jit(solution)/shard_map/all_to_all | solution.py:336
  91.7 0.8 suffix.1
  92.6 4.7 %all-to-all-start.4 = ((f32[32,32,128]{2,1,0:T(8,128)}), f32[32,32,128]{2,1,0:T(8,128)S(1)}, u32[]{:S(2)}, u32[]{:S(2)}) async-start(f32[32,32,128]{2,1,0:T(8,128)} %get-tuple-element.49._), calls=%async_computation.4 | async-start | bytes 1048576 | tf_op jit(solution)/shard_map/all_to_all | solution.py:354
  97.3 1.9 %collective-permute-start = (f32[8,128]{1,0:T(8,128)S(1)}, f32[8,128]{1,0:T(8,128)S(1)}, u32[]{:S(2)}, u32[]{:S(2)}) collective-permute-start(f32[8,128]{1,0:T(8,128)S(1)} %get-tuple-element.48.gain_a), channel_id=1, source_target_pairs={{0,1},{1,0},{2,3},{3,2},{4,5},{5,4},{6,7},{7,6},{8,9},{9,8},{10,11... | collective-permute-start | bytes 12296 | tf_op jit(solution)/shard_map/ppermute | solution.py:355
  99.2 1.1 collective-permute-done.gain_b
  100.4 2.4 %return_operands.1 = (bf16[256,1024]{1,0:T(8,128)(2,1)S(1)}, bf16[256,512]{1,0:T(8,128)(2,1)S(1)}, f32[256,1024]{1,0:T(8,128)S(1)}, f32[256,1024]{1,0:T(8,128)S(1)}, f32[8,128]{1,0:T(8,128)}) custom-call(bf16[256,1024]{1,0:T(8,128)(2,1)} %bitcast.25, bf16[256,1024]{1,0:T(8,128)(2,1)} %bitcast.20, f32[256,1024]{1,0:T(8,128)} %get-tuple-element.45.dk_hbm, ...), custom_call_target="tpu_custom_call" | custom-call | flops 131072 | bytes 6565888 | tf_op jit(solution)/shard_map/return_operands/pallas_call | solution.py:47
  102.8 8.5 %all-to-all-done.4 = f32[32,32,128]{2,1,0:T(8,128)S(1)} async-done(((f32[32,32,128]{2,1,0:T(8,128)}), f32[32,32,128]{2,1,0:T(8,128)S(1)}, u32[]{:S(2)}, u32[]{:S(2)}) %all-to-all-start.4) | async-done | bytes 524320 | tf_op jit(solution)/shard_map/all_to_all | solution.py:354
  111.3 2.0 %key_value_gradients.1 = (bf16[256,1024]{1,0:T(8,128)(2,1)}, bf16[256,1024]{1,0:T(8,128)(2,1)}) custom-call(bf16[256,1024]{1,0:T(8,128)(2,1)S(1)} %get-tuple-element.50.k_ref, bf16[256,512]{1,0:T(8,128)(2,1)S(1)} %get-tuple-element.51.v_near, bf16[256,1024]{1,0:T(8,128)(2,1)} %bitcast.21, f32[1024,128]{1,0:T(8,128)S(1)} %bitcast.15, ...), custom_call_target="tpu_custom_call" | custom-call | flops 268435456 | bytes 4980736 | tf_op jit(solution)/shard_map/key_value_gradients/pallas_call | solution.py:47
Async XLA Ops:
  33.1 20.1 %all-to-all-start.1 = ((f32[32,32,128]{2,1,0:T(8,128)}), f32[32,32,128]{2,1,0:T(8,128)S(1)}, u32[]{:S(2)}, u32[]{:S(2)}) async-start(f32[32,32,128]{2,1,0:T(8,128)} %prefix.1), calls=%async_computation.1 | async-start | bytes 1048576 | tf_op jit(solution)/shard_map/all_to_all | solution.py:319
  53.8 16.9 %copy-start = (f32[256,1024]{1,0:T(8,128)}, f32[256,1024]{1,0:T(8,128)S(1)}, u32[]{:S(2)}) copy-start(f32[256,1024]{1,0:T(8,128)S(1)} %get-tuple-element.40.attn_ref) | copy-start | bytes 3145732
  70.7 5.0 %copy-start.1 = (f32[256,1024]{1,0:T(8,128)S(1)}, f32[256,1024]{1,0:T(8,128)}, u32[]{:S(2)}) copy-start(f32[256,1024]{1,0:T(8,128)} %copy-done) | copy-start | bytes 3145732
  70.7 21.0 %all-to-all-start.3 = ((f32[32,40,128]{2,1,0:T(8,128)}), f32[32,40,128]{2,1,0:T(8,128)S(1)}, u32[]{:S(2)}, u32[]{:S(2)}) async-start(f32[32,40,128]{2,1,0:T(8,128)} %get-tuple-element.47), calls=%async_computation.3 | async-start | bytes 1310720 | tf_op jit(solution)/shard_map/all_to_all | solution.py:336
  92.6 18.7 %all-to-all-start.4 = ((f32[32,32,128]{2,1,0:T(8,128)}), f32[32,32,128]{2,1,0:T(8,128)S(1)}, u32[]{:S(2)}, u32[]{:S(2)}) async-start(f32[32,32,128]{2,1,0:T(8,128)} %get-tuple-element.49._), calls=%async_computation.4 | async-start | bytes 1048576 | tf_op jit(solution)/shard_map/all_to_all | solution.py:354
  97.3 3.1 %collective-permute-start = (f32[8,128]{1,0:T(8,128)S(1)}, f32[8,128]{1,0:T(8,128)S(1)}, u32[]{:S(2)}, u32[]{:S(2)}) collective-permute-start(f32[8,128]{1,0:T(8,128)S(1)} %get-tuple-element.48.gain_a), channel_id=1, source_target_pairs={{0,1},{1,0},{2,3},{3,2},{4,5},{5,4},{6,7},{7,6},{8,9},{9,8},{10,11... | collective-permute-start | bytes 12296 | tf_op jit(solution)/shard_map/ppermute | solution.py:355

commit v3 on v2

--- a/solution.py
+++ b/solution.py
@@ -76,27 +76,15 @@
 
 
 def states_kernel(q_hbm, k_hbm, v_hbm, dy_hbm, gain_hbm, state_ref, within_ref, q_ref, dy_ref, gain_ref, k_ref, v_ref, sems):
-    first = lax.axis_index("dp") == 0
-    near = fetch(((k_hbm, k_ref), (v_hbm, v_ref)), sems)
-    later = [
-        pltpu.make_async_copy(src, dst, sems.at[2 + i])
-        for i, (src, dst) in enumerate(((q_hbm, q_ref), (dy_hbm, dy_ref), (gain_hbm, gain_ref)))
-    ]
-
-    @pl.when(first)
+    for copy in fetch(((k_hbm, k_ref), (v_hbm, v_ref)), sems):
+        copy.wait()
+    for head in range(k_ref.shape[1] // DH):
+        at = columns(head)
+        state_ref[at, :] = dot(k_ref[:, at], v_ref[:, at], 0, 0)
+
+    @pl.when(lax.axis_index("dp") == 0)
     def _():
-        for copy in later:
-            copy.start()
-
-    for copy in near:
-        copy.wait()
-    for head in range(k_ref.shape[1] // DH):
-        at = columns(head)
-        state_ref[at, :] = dot(k_ref[:, at], v_ref[:, at], 0, 0)
-
-    @pl.when(first)
-    def _():
-        for copy in later:
+        for copy in fetch(((q_hbm, q_ref), (dy_hbm, dy_ref), (gain_hbm, gain_ref)), sems):
             copy.wait()
         attend_within(q_ref, k_ref, v_ref, within_ref)
 

time: 114 us -> 111 us (0.974)
  waiting for transfers between devices: 33.6 us -> 31.5 us
  Pallas kernels: 18.9 us -> 20.1 us
    pallas_call x9, Pallas kernels: 18.9 us -> 20.1 us  [call(): pl.pallas_call(kernel, name=name, in_specs=[spec(w) for _, w in ins], out...]
  transfers between devices with their start and end apart: 4 -> 4, of which waited for: 4 -> 4; matrix products, arithmetic and copies ran while one was open for 0% -> 0% of each run, Pallas kernels for 8% -> 9%
where the time goes in v3:
time: 111 us; the launch traced here: 110 us
  blocking collectives  42.5 us (38%)
  waiting for transfers between devices  31.5 us (28%)
  Pallas kernels  20.1 us (18%)
  starting transfers between devices  15.6 us (14%)
    all_to_all x1, blocking collectives, body(): parts = exchange(local).reshape(ctx, rows, DH)  27.2 us
    pallas_call x9, Pallas kernels, call(): pl.pallas_call(kernel, name=name, in_specs=[spec(w) for _, w in ins], out...  20.1 us
    all_to_all x1, blocking collectives, body(): sums = lax.all_to_all(sums, 'heads', 0, 0, tiled=True)  15.3 us
    all_to_all x1, waiting for transfers between devices, body(): prefix = exchange(before.reshape(wide, DH))  14.2 us
    all_to_all x1, waiting for transfers between devices, body(): grad_parts = exchange(grad_local)  8.17 us
    all_to_all x1, waiting for transfers between devices, body(): suffix = exchange(after.reshape(wide, DH))  7.95 us
    all_to_all x1, starting transfers between devices, body(): prefix = exchange(before.reshape(wide, DH))  4.67 us
    all_to_all x1, starting transfers between devices, body(): grad_parts = exchange(grad_local)  4.54 us
  transfers between devices with their start and end apart: 4, of which 4 were waited for; matrix products, arithmetic and copies ran while one was open for 0% of the time, Pallas kernels for 9%

profile of v3, /device:TPU:64, one launch (start us, length us, event | category | flops | bytes accessed | tf_op | source)
XLA Modules:
  0.0 110.4 jit_solution(11480698284403303232)
XLA Ops:
  0.6 4.6 %key_value_states.1 = (f32[1024,128]{1,0:T(8,128)S(1)}, f32[256,1024]{1,0:T(8,128)S(1)}, bf16[256,1024]{1,0:T(8,128)(2,1)S(1)}, bf16[256,1024]{1,0:T(8,128)(2,1)S(1)}, f32[1,1024]{1,0:T(1,128)S(1)}) custom-call(bf16[256,1024]{1,0:T(8,128)(2,1)} %bitcast.26, bf16[256,1024]{1,0:T(8,128)(2,1)} %bitcast.22, bf16[256,1024]{1,0:T(8,128)(2,1)} %bitcast.17, ...), custom_call_target="tpu_custom_call" | custom-call | flops 268435456 | bytes 4726784 | tf_op jit(solution)/shard_map/key_value_states/pallas_call | solution.py:47
  5.2 27.2 %all_to_all.35.part_ref = f32[32,32,128]{2,1,0:T(8,128)S(1)} all-to-all(f32[32,32,128]{2,1,0:T(8,128)S(1)} %bitcast.16), channel_id=1, replica_groups=mesh['ctx'=32,'heads'=8,'dp'=2] {'ctx'}, dimensions={0} | all-to-all | bytes 1048576 | tf_op jit(solution)/shard_map/all_to_all | solution.py:293
  32.5 0.8 prefix.1
  33.3 4.7 %all-to-all-start.1 = ((f32[32,32,128]{2,1,0:T(8,128)}), f32[32,32,128]{2,1,0:T(8,128)S(1)}, u32[]{:S(2)}, u32[]{:S(2)}) async-start(f32[32,32,128]{2,1,0:T(8,128)} %prefix.1), calls=%async_computation.1 | async-start | bytes 1048576 | tf_op jit(solution)/shard_map/all_to_all | solution.py:307
  38.0 0.1 within_block.1
  38.0 14.2 %all-to-all-done.1 = f32[32,32,128]{2,1,0:T(8,128)S(1)} async-done(((f32[32,32,128]{2,1,0:T(8,128)}), f32[32,32,128]{2,1,0:T(8,128)S(1)}, u32[]{:S(2)}, u32[]{:S(2)}) %all-to-all-start.1) | async-done | bytes 524320 | tf_op jit(solution)/shard_map/all_to_all | solution.py:307
  52.3 0.6 attend.1
  52.9 0.0 copy-start
  52.9 15.3 %all_to_all.36.sums_ref = f32[8,8,256]{2,1,0:T(8,128)S(1)} all-to-all(f32[8,8,256]{2,1,0:T(8,128)S(1)} %get-tuple-element.41), channel_id=1, replica_groups=mesh['ctx'=32,'heads'=8,'dp'=2] {'heads'}, dimensions={0} | all-to-all | bytes 131072 | tf_op jit(solution)/shard_map/all_to_all | solution.py:315
  68.2 1.6 %grad_states.1 = (f32[32,40,128]{2,1,0:T(8,128)}, f32[2,256,128]{2,1,0:T(8,128)S(1)}) custom-call(f32[8,8,256]{2,1,0:T(8,128)S(1)} %all_to_all.36.sums_ref, bf16[256,1024]{1,0:T(8,128)(2,1)S(1)} %get-tuple-element.36.q_ref, f32[256,1024]{1,0:T(8,128)S(1)} %get-tuple-element.40.attn_ref, f32[1,1024]{1,0:T(1,128)S(1)} %get-tuple-element.35.gain_ref, ...), custom_call_target="tpu_custom_call" | custom-call | flops 134217728 | bytes 3084288 | tf_op jit(solution)/shard_map/grad_states/pallas_call | solution.py:47
  69.8 0.0 copy-done
  69.8 0.0 copy-start.1
  69.8 4.5 %all-to-all-start.3 = ((f32[32,40,128]{2,1,0:T(8,128)}), f32[32,40,128]{2,1,0:T(8,128)S(1)}, u32[]{:S(2)}, u32[]{:S(2)}) async-start(f32[32,40,128]{2,1,0:T(8,128)} %get-tuple-element.47), calls=%async_computation.3 | async-start | bytes 1310720 | tf_op jit(solution)/shard_map/all_to_all | solution.py:324
  74.4 0.0 copy-done.1
  74.4 7.1 %backward_within.1 = (bf16[256,1024]{1,0:T(8,128)(2,1)}, bf16[256,1024]{1,0:T(8,128)(2,1)}, f32[256,1024]{1,0:T(8,128)}, f32[256,1024]{1,0:T(8,128)}) custom-call(bf16[256,1024]{1,0:T(8,128)(2,1)} %bitcast.28, bf16[256,1024]{1,0:T(8,128)(2,1)} %bitcast.24, bf16[256,1024]{1,0:T(8,128)(2,1)} %bitcast.19, bf16[256,1024]{1,0:T(8,128)(2,1)} %bitcast.31, ...), custom_call_target="tpu_custom_call" | custom-call | flops 1476395008 | bytes 7081984 | tf_op jit(solution)/shard_map/backward_within/pallas_call | solution.py:47
  81.5 8.2 %all-to-all-done.3.part_ref = f32[32,40,128]{2,1,0:T(8,128)S(1)} async-done(((f32[32,40,128]{2,1,0:T(8,128)}), f32[32,40,128]{2,1,0:T(8,128)S(1)}, u32[]{:S(2)}, u32[]{:S(2)}) %all-to-all-start.3) | async-done | bytes 655392 | tf_op jit(solution)/shard_map/all_to_all | solution.py:324
  89.7 0.8 suffix.1
  90.5 4.5 %all-to-all-start.4 = ((f32[32,32,128]{2,1,0:T(8,128)}), f32[32,32,128]{2,1,0:T(8,128)S(1)}, u32[]{:S(2)}, u32[]{:S(2)}) async-start(f32[32,32,128]{2,1,0:T(8,128)} %get-tuple-element.49._), calls=%async_computation.4 | async-start | bytes 1048576 | tf_op jit(solution)/shard_map/all_to_all | solution.py:342
  95.0 1.9 %collective-permute-start = (f32[8,128]{1,0:T(8,128)S(1)}, f32[8,128]{1,0:T(8,128)S(1)}, u32[]{:S(2)}, u32[]{:S(2)}) collective-permute-start(f32[8,128]{1,0:T(8,128)S(1)} %get-tuple-element.48.gain_a), channel_id=1, source_target_pairs={{0,1},{1,0},{2,3},{3,2},{4,5},{5,4},{6,7},{7,6},{8,9},{9,8},{10,11... | collective-permute-start | bytes 12296 | tf_op jit(solution)/shard_map/ppermute | solution.py:343
  96.9 1.1 %collective-permute-done.gain_b = f32[8,128]{1,0:T(8,128)S(1)} collective-permute-done((f32[8,128]{1,0:T(8,128)S(1)}, f32[8,128]{1,0:T(8,128)S(1)}, u32[]{:S(2)}, u32[]{:S(2)}) %collective-permute-start) | collective-permute-done | bytes 4128 | tf_op jit(solution)/shard_map/ppermute | solution.py:343
  98.1 2.4 %return_operands.1 = (bf16[256,1024]{1,0:T(8,128)(2,1)S(1)}, bf16[256,512]{1,0:T(8,128)(2,1)S(1)}, f32[256,1024]{1,0:T(8,128)S(1)}, f32[256,1024]{1,0:T(8,128)S(1)}, f32[8,128]{1,0:T(8,128)}) custom-call(bf16[256,1024]{1,0:T(8,128)(2,1)} %bitcast.25, bf16[256,1024]{1,0:T(8,128)(2,1)} %bitcast.20, f32[256,1024]{1,0:T(8,128)} %get-tuple-element.45.dk_hbm, ...), custom_call_target="tpu_custom_call" | custom-call | flops 131072 | bytes 6565888 | tf_op jit(solution)/shard_map/return_operands/pallas_call | solution.py:47
  100.5 8.0 %all-to-all-done.4 = f32[32,32,128]{2,1,0:T(8,128)S(1)} async-done(((f32[32,32,128]{2,1,0:T(8,128)}), f32[32,32,128]{2,1,0:T(8,128)S(1)}, u32[]{:S(2)}, u32[]{:S(2)}) %all-to-all-start.4) | async-done | bytes 524320 | tf_op jit(solution)/shard_map/all_to_all | solution.py:342
  108.4 2.0 %key_value_gradients.1 = (bf16[256,1024]{1,0:T(8,128)(2,1)}, bf16[256,1024]{1,0:T(8,128)(2,1)}) custom-call(bf16[256,1024]{1,0:T(8,128)(2,1)S(1)} %get-tuple-element.50.k_ref, bf16[256,512]{1,0:T(8,128)(2,1)S(1)} %get-tuple-element.51.v_near, bf16[256,1024]{1,0:T(8,128)(2,1)} %bitcast.21, f32[1024,128]{1,0:T(8,128)S(1)} %bitcast.15, ...), custom_call_target="tpu_custom_call" | custom-call | flops 268435456 | bytes 4980736 | tf_op jit(solution)/shard_map/key_value_gradients/pallas_call | solution.py:47
Async XLA Ops:
  33.3 19.0 %all-to-all-start.1 = ((f32[32,32,128]{2,1,0:T(8,128)}), f32[32,32,128]{2,1,0:T(8,128)S(1)}, u32[]{:S(2)}, u32[]{:S(2)}) async-start(f32[32,32,128]{2,1,0:T(8,128)} %prefix.1), calls=%async_computation.1 | async-start | bytes 1048576 | tf_op jit(solution)/shard_map/all_to_all | solution.py:307
  52.9 16.9 %copy-start = (f32[256,1024]{1,0:T(8,128)}, f32[256,1024]{1,0:T(8,128)S(1)}, u32[]{:S(2)}) copy-start(f32[256,1024]{1,0:T(8,128)S(1)} %get-tuple-element.40.attn_ref) | copy-start | bytes 3145732
  69.8 4.6 %copy-start.1 = (f32[256,1024]{1,0:T(8,128)S(1)}, f32[256,1024]{1,0:T(8,128)}, u32[]{:S(2)}) copy-start(f32[256,1024]{1,0:T(8,128)} %copy-done) | copy-start | bytes 3145732
  69.8 19.9 %all-to-all-start.3 = ((f32[32,40,128]{2,1,0:T(8,128)}), f32[32,40,128]{2,1,0:T(8,128)S(1)}, u32[]{:S(2)}, u32[]{:S(2)}) async-start(f32[32,40,128]{2,1,0:T(8,128)} %get-tuple-element.47), calls=%async_computation.3 | async-start | bytes 1310720 | tf_op jit(solution)/shard_map/all_to_all | solution.py:324
  90.5 17.9 %all-to-all-start.4 = ((f32[32,32,128]{2,1,0:T(8,128)}), f32[32,32,128]{2,1,0:T(8,128)S(1)}, u32[]{:S(2)}, u32[]{:S(2)}) async-start(f32[32,32,128]{2,1,0:T(8,128)} %get-tuple-element.49._), calls=%async_computation.4 | async-start | bytes 1048576 | tf_op jit(solution)/shard_map/all_to_all | solution.py:342
  95.0 3.1 %collective-permute-start = (f32[8,128]{1,0:T(8,128)S(1)}, f32[8,128]{1,0:T(8,128)S(1)}, u32[]{:S(2)}, u32[]{:S(2)}) collective-permute-start(f32[8,128]{1,0:T(8,128)S(1)} %get-tuple-element.48.gain_a), channel_id=1, source_target_pairs={{0,1},{1,0},{2,3},{3,2},{4,5},{5,4},{6,7},{7,6},{8,9},{9,8},{10,11... | collective-permute-start | bytes 12296 | tf_op jit(solution)/shard_map/ppermute | solution.py:343

commit v4 on v3

--- a/solution.py
+++ b/solution.py
@@ -147,12 +147,11 @@
         attn_ref[:, at] = attn
         squares += attn * attn
         inner += (gain_ref[:, at] * dy_ref[:, at].astype(F32)) * attn
-    row = lax.broadcasted_iota(jnp.int32, (8, tokens), 0)
-    sums = jnp.where(
-        row == 0,
-        jnp.sum(squares.T, axis=0, keepdims=True),
-        jnp.where(row == 1, jnp.sum(inner.T, axis=0, keepdims=True), 0.0),
-    )
+    rows = []
+    for total in (squares, inner):
+        line = jnp.sum(total.T, axis=0, keepdims=True)
+        rows += [line[:, i : i + DH] for i in range(0, tokens, DH)]
+    sums = jnp.concatenate(rows, 0)
     for i in range(sums_ref.shape[0]):
         sums_ref[i] = sums
 
@@ -161,11 +160,15 @@
     sums = sums_ref[0]
     for i in range(1, sums_ref.shape[0]):
         sums = sums + sums_ref[i]
-    inverse = 1.0 / jnp.sqrt(sums[0:1] / width + epsilon)
-    other = sums[1:2] * (inverse * inverse * inverse) / width
-    row = lax.broadcasted_iota(jnp.int32, sums.shape, 0)
-    both = jnp.where(row == 0, inverse, other).T
-    return tuple(jnp.broadcast_to(both[:, i : i + 1], (both.shape[0], DH)) for i in range(2))
+    count = sums.shape[0] // 2
+    inverse = 1.0 / jnp.sqrt(sums[:count] / width + epsilon)
+    other = sums[count:] * (inverse * inverse * inverse) / width
+    both = jnp.concatenate([inverse, other, jnp.zeros((8 - 2 * count, DH), F32)], 0).T
+
+    def spread(first):
+        return jnp.concatenate([jnp.broadcast_to(both[:, i : i + 1], (DH, DH)) for i in range(first, first + count)], 0)
+
+    return spread(0), spread(count)
 
 
 def grad_state_kernel(width, sums_ref, q_ref, attn_ref, gain_ref, dy_ref, state_hbm, factor_ref, state_ref, sems):
@@ -309,7 +312,7 @@
         functools.partial(attend_kernel, scale),
         "attend",
         [(q_near, "vmem"), (within, "vmem"), (prefix, ""), (gain_near, "vmem"), (dy_near, "vmem")],
-        [(all_tok, F32, "vmem"), ((shards, 8, tokens), F32, "")],
+        [(all_tok, F32, "vmem"), ((shards, 2 * tokens // DH, DH), F32, "")],
         2 * per,
     )
     sums = lax.all_to_all(sums, "heads", 0, 0, tiled=True)

time: 111 us -> 110 us (level)
  no operation moved by 1% of the time
where the time goes in v4:
time: 110 us
  blocking collectives  41.9 us (38%)
  waiting for transfers between devices  31.5 us (29%)
  Pallas kernels  20.1 us (18%)
  starting transfers between devices  15.6 us (14%)
    all_to_all x1, blocking collectives, body(): parts = exchange(local).reshape(ctx, rows, DH)  27.2 us
    pallas_call x9, Pallas kernels, call(): pl.pallas_call(kernel, name=name, in_specs=[spec(w) for _, w in ins], out...  20.1 us
    all_to_all x1, blocking collectives, body(): sums = lax.all_to_all(sums, 'heads', 0, 0, tiled=True)  14.7 us
    all_to_all x1, waiting for transfers between devices, body(): prefix = exchange(before.reshape(wide, DH))  14.2 us
    all_to_all x1, waiting for transfers between devices, body(): grad_parts = exchange(grad_local)  8.17 us
    all_to_all x1, waiting for transfers between devices, body(): suffix = exchange(after.reshape(wide, DH))  7.95 us
    all_to_all x1, starting transfers between devices, body(): prefix = exchange(before.reshape(wide, DH))  4.67 us
    all_to_all x1, starting transfers between devices, body(): grad_parts = exchange(grad_local)  4.54 us
  transfers between devices with their start and end apart: 4, of which 4 were waited for; matrix products, arithmetic and copies ran while one was open for 0% of the time, Pallas kernels for 9%

profile of v4, /device:TPU:64, one launch (start us, length us, event | category | flops | bytes accessed | tf_op | source)
XLA Modules:
  0.0 109.8 jit_solution(13987507600886344825)
XLA Ops:
  0.6 4.6 %key_value_states.1 = (f32[1024,128]{1,0:T(8,128)S(1)}, f32[256,1024]{1,0:T(8,128)S(1)}, bf16[256,1024]{1,0:T(8,128)(2,1)S(1)}, bf16[256,1024]{1,0:T(8,128)(2,1)S(1)}, f32[1,1024]{1,0:T(1,128)S(1)}) custom-call(bf16[256,1024]{1,0:T(8,128)(2,1)} %bitcast.26, bf16[256,1024]{1,0:T(8,128)(2,1)} %bitcast.22, bf16[256,1024]{1,0:T(8,128)(2,1)} %bitcast.17, ...), custom_call_target="tpu_custom_call" | custom-call | flops 268435456 | bytes 4726784 | tf_op jit(solution)/shard_map/key_value_states/pallas_call | solution.py:47
  5.2 27.2 %all_to_all.35.part_ref = f32[32,32,128]{2,1,0:T(8,128)S(1)} all-to-all(f32[32,32,128]{2,1,0:T(8,128)S(1)} %bitcast.16), channel_id=1, replica_groups=mesh['ctx'=32,'heads'=8,'dp'=2] {'ctx'}, dimensions={0} | all-to-all | bytes 1048576 | tf_op jit(solution)/shard_map/all_to_all | solution.py:296
  32.5 0.8 prefix.1
  33.3 4.7 %all-to-all-start.1 = ((f32[32,32,128]{2,1,0:T(8,128)}), f32[32,32,128]{2,1,0:T(8,128)S(1)}, u32[]{:S(2)}, u32[]{:S(2)}) async-start(f32[32,32,128]{2,1,0:T(8,128)} %prefix.1), calls=%async_computation.1 | async-start | bytes 1048576 | tf_op jit(solution)/shard_map/all_to_all | solution.py:310
  38.0 0.1 within_block.1
  38.0 14.2 %all-to-all-done.1 = f32[32,32,128]{2,1,0:T(8,128)S(1)} async-done(((f32[32,32,128]{2,1,0:T(8,128)}), f32[32,32,128]{2,1,0:T(8,128)S(1)}, u32[]{:S(2)}, u32[]{:S(2)}) %all-to-all-start.1) | async-done | bytes 524320 | tf_op jit(solution)/shard_map/all_to_all | solution.py:310
  52.3 0.6 attend.1
  52.9 0.0 copy-start
  52.9 14.7 %all_to_all.36.sums_ref = f32[8,4,128]{2,1,0:T(4,128)S(1)} all-to-all(f32[8,4,128]{2,1,0:T(4,128)S(1)} %get-tuple-element.41), channel_id=1, replica_groups=mesh['ctx'=32,'heads'=8,'dp'=2] {'heads'}, dimensions={0} | all-to-all | bytes 32768 | tf_op jit(solution)/shard_map/all_to_all | solution.py:318
  67.5 1.6 %grad_states.1 = (f32[32,40,128]{2,1,0:T(8,128)}, f32[2,256,128]{2,1,0:T(8,128)S(1)}) custom-call(f32[8,4,128]{2,1,0:T(4,128)S(1)} %all_to_all.36.sums_ref, bf16[256,1024]{1,0:T(8,128)(2,1)S(1)} %get-tuple-element.36.q_ref, f32[256,1024]{1,0:T(8,128)S(1)} %get-tuple-element.40.attn_ref, f32[1,1024]{1,0:T(1,128)S(1)} %get-tuple-element.35.gain_ref, ...), custom_call_target="tpu_custom_call" | custom-call | flops 134217728 | bytes 3035136 | tf_op jit(solution)/shard_map/grad_states/pallas_call | solution.py:47
  69.2 0.0 copy-done
  69.2 0.0 copy-start.1
  69.2 4.5 %all-to-all-start.3 = ((f32[32,40,128]{2,1,0:T(8,128)}), f32[32,40,128]{2,1,0:T(8,128)S(1)}, u32[]{:S(2)}, u32[]{:S(2)}) async-start(f32[32,40,128]{2,1,0:T(8,128)} %get-tuple-element.47), calls=%async_computation.3 | async-start | bytes 1310720 | tf_op jit(solution)/shard_map/all_to_all | solution.py:327
  73.7 0.0 copy-done.1
  73.7 7.1 %backward_within.1 = (bf16[256,1024]{1,0:T(8,128)(2,1)}, bf16[256,1024]{1,0:T(8,128)(2,1)}, f32[256,1024]{1,0:T(8,128)}, f32[256,1024]{1,0:T(8,128)}) custom-call(bf16[256,1024]{1,0:T(8,128)(2,1)} %bitcast.28, bf16[256,1024]{1,0:T(8,128)(2,1)} %bitcast.24, bf16[256,1024]{1,0:T(8,128)(2,1)} %bitcast.19, bf16[256,1024]{1,0:T(8,128)(2,1)} %bitcast.31, ...), custom_call_target="tpu_custom_call" | custom-call | flops 1476395008 | bytes 7081984 | tf_op jit(solution)/shard_map/backward_within/pallas_call | solution.py:47
  80.9 8.2 %all-to-all-done.3.part_ref = f32[32,40,128]{2,1,0:T(8,128)S(1)} async-done(((f32[32,40,128]{2,1,0:T(8,128)}), f32[32,40,128]{2,1,0:T(8,128)S(1)}, u32[]{:S(2)}, u32[]{:S(2)}) %all-to-all-start.3) | async-done | bytes 655392 | tf_op jit(solution)/shard_map/all_to_all | solution.py:327
  89.1 0.8 suffix.1
  89.9 4.5 %all-to-all-start.4 = ((f32[32,32,128]{2,1,0:T(8,128)}), f32[32,32,128]{2,1,0:T(8,128)S(1)}, u32[]{:S(2)}, u32[]{:S(2)}) async-start(f32[32,32,128]{2,1,0:T(8,128)} %get-tuple-element.49._), calls=%async_computation.4 | async-start | bytes 1048576 | tf_op jit(solution)/shard_map/all_to_all | solution.py:345
  94.4 1.9 %collective-permute-start = (f32[8,128]{1,0:T(8,128)S(1)}, f32[8,128]{1,0:T(8,128)S(1)}, u32[]{:S(2)}, u32[]{:S(2)}) collective-permute-start(f32[8,128]{1,0:T(8,128)S(1)} %get-tuple-element.48.gain_a), channel_id=1, source_target_pairs={{0,1},{1,0},{2,3},{3,2},{4,5},{5,4},{6,7},{7,6},{8,9},{9,8},{10,11... | collective-permute-start | bytes 12296 | tf_op jit(solution)/shard_map/ppermute | solution.py:346
  96.3 1.1 %collective-permute-done.gain_b = f32[8,128]{1,0:T(8,128)S(1)} collective-permute-done((f32[8,128]{1,0:T(8,128)S(1)}, f32[8,128]{1,0:T(8,128)S(1)}, u32[]{:S(2)}, u32[]{:S(2)}) %collective-permute-start) | collective-permute-done | bytes 4128 | tf_op jit(solution)/shard_map/ppermute | solution.py:346
  97.4 2.4 %return_operands.1 = (bf16[256,1024]{1,0:T(8,128)(2,1)S(1)}, bf16[256,512]{1,0:T(8,128)(2,1)S(1)}, f32[256,1024]{1,0:T(8,128)S(1)}, f32[256,1024]{1,0:T(8,128)S(1)}, f32[8,128]{1,0:T(8,128)}) custom-call(bf16[256,1024]{1,0:T(8,128)(2,1)} %bitcast.25, bf16[256,1024]{1,0:T(8,128)(2,1)} %bitcast.20, f32[256,1024]{1,0:T(8,128)} %get-tuple-element.45.dk_hbm, ...), custom_call_target="tpu_custom_call" | custom-call | flops 131072 | bytes 6565888 | tf_op jit(solution)/shard_map/return_operands/pallas_call | solution.py:47
  99.8 8.0 %all-to-all-done.4 = f32[32,32,128]{2,1,0:T(8,128)S(1)} async-done(((f32[32,32,128]{2,1,0:T(8,128)}), f32[32,32,128]{2,1,0:T(8,128)S(1)}, u32[]{:S(2)}, u32[]{:S(2)}) %all-to-all-start.4) | async-done | bytes 524320 | tf_op jit(solution)/shard_map/all_to_all | solution.py:345
  107.8 2.0 %key_value_gradients.1 = (bf16[256,1024]{1,0:T(8,128)(2,1)}, bf16[256,1024]{1,0:T(8,128)(2,1)}) custom-call(bf16[256,1024]{1,0:T(8,128)(2,1)S(1)} %get-tuple-element.50.k_ref, bf16[256,512]{1,0:T(8,128)(2,1)S(1)} %get-tuple-element.51.v_near, bf16[256,1024]{1,0:T(8,128)(2,1)} %bitcast.21, f32[1024,128]{1,0:T(8,128)S(1)} %bitcast.15, ...), custom_call_target="tpu_custom_call" | custom-call | flops 268435456 | bytes 4980736 | tf_op jit(solution)/shard_map/key_value_gradients/pallas_call | solution.py:47
Async XLA Ops:
  33.3 19.0 %all-to-all-start.1 = ((f32[32,32,128]{2,1,0:T(8,128)}), f32[32,32,128]{2,1,0:T(8,128)S(1)}, u32[]{:S(2)}, u32[]{:S(2)}) async-start(f32[32,32,128]{2,1,0:T(8,128)} %prefix.1), calls=%async_computation.1 | async-start | bytes 1048576 | tf_op jit(solution)/shard_map/all_to_all | solution.py:310
  52.9 16.3 %copy-start = (f32[256,1024]{1,0:T(8,128)}, f32[256,1024]{1,0:T(8,128)S(1)}, u32[]{:S(2)}) copy-start(f32[256,1024]{1,0:T(8,128)S(1)} %get-tuple-element.40.attn_ref) | copy-start | bytes 3145732
  69.2 4.6 %copy-start.1 = (f32[256,1024]{1,0:T(8,128)S(1)}, f32[256,1024]{1,0:T(8,128)}, u32[]{:S(2)}) copy-start(f32[256,1024]{1,0:T(8,128)} %copy-done) | copy-start | bytes 3145732
  69.2 19.9 %all-to-all-start.3 = ((f32[32,40,128]{2,1,0:T(8,128)}), f32[32,40,128]{2,1,0:T(8,128)S(1)}, u32[]{:S(2)}, u32[]{:S(2)}) async-start(f32[32,40,128]{2,1,0:T(8,128)} %get-tuple-element.47), calls=%async_computation.3 | async-start | bytes 1310720 | tf_op jit(solution)/shard_map/all_to_all | solution.py:327
  89.9 17.9 %all-to-all-start.4 = ((f32[32,32,128]{2,1,0:T(8,128)}), f32[32,32,128]{2,1,0:T(8,128)S(1)}, u32[]{:S(2)}, u32[]{:S(2)}) async-start(f32[32,32,128]{2,1,0:T(8,128)} %get-tuple-element.49._), calls=%async_computation.4 | async-start | bytes 1048576 | tf_op jit(solution)/shard_map/all_to_all | solution.py:345
  94.4 3.1 %collective-permute-start = (f32[8,128]{1,0:T(8,128)S(1)}, f32[8,128]{1,0:T(8,128)S(1)}, u32[]{:S(2)}, u32[]{:S(2)}) collective-permute-start(f32[8,128]{1,0:T(8,128)S(1)} %get-tuple-element.48.gain_a), channel_id=1, source_target_pairs={{0,1},{1,0},{2,3},{3,2},{4,5},{5,4},{6,7},{7,6},{8,9},{9,8},{10,11... | collective-permute-start | bytes 12296 | tf_op jit(solution)/shard_map/ppermute | solution.py:346

commit v5 on v4

--- a/solution.py
+++ b/solution.py
@@ -68,11 +68,14 @@
 
 
 def attend_within(q_ref, k_ref, v_ref, within_ref):
-    for head in range(q_ref.shape[1] // DH):
-        at = columns(head)
+    def one(head, _):
+        at = pl.ds(pl.multiple_of(head * DH, DH), DH)
         upper, lower = halves(causal(dot(q_ref[:, at], k_ref[:, at], 1, 1)))
         v = v_ref[:, at]
         within_ref[:, at] = dot(upper, v) + dot(lower, v)
+        return 0
+
+    lax.fori_loop(0, q_ref.shape[1] // DH, one, 0)
 
 
 def states_kernel(q_hbm, k_hbm, v_hbm, dy_hbm, gain_hbm, state_ref, within_ref, q_ref, dy_ref, gain_ref, k_ref, v_ref, sems):
@@ -233,23 +236,23 @@
 
 
 def return_kernel(k_hbm, v_hbm, dk_hbm, dv_hbm, gain_a, gain_b, _, k_ref, v_ref, dk_ref, dv_ref, gain_ref, sems):
-    v_half = v_hbm.at[:, pl.ds(0, v_ref.shape[1])]
-    copies = fetch(((k_hbm, k_ref), (v_half, v_ref), (dk_hbm, dk_ref), (dv_hbm, dv_ref)), sems)
+    dk_first = dk_hbm.at[:, pl.ds(0, dk_ref.shape[1])]
+    copies = fetch(((k_hbm, k_ref), (v_hbm, v_ref), (dk_first, dk_ref), (dv_hbm, dv_ref)), sems)
     gain_ref[...] = gain_a[...] + gain_b[...]
     for copy in copies:
         copy.wait()
 
 
-def last_kernel(scale, k_ref, v_near, v_hbm, state_ref, dk_in, dv_in, dk_hbm, dv_hbm, v_far, dk_ref, dv_ref, sems):
-    wide = v_near.shape[1]
+def last_kernel(scale, k_ref, v_ref, state_ref, dk_near, dk_part, dv_in, dk_hbm, dv_hbm, dk_far, dk_ref, dv_ref, sems):
     heads = k_ref.shape[1] // DH
+    near = dk_near.shape[1] // DH
     half = heads // 2
-    v_copy = pltpu.make_async_copy(v_hbm.at[:, pl.ds(wide, wide)], v_far, sems.at[4])
-    v_copy.start()
+    far_copy = pltpu.make_async_copy(dk_part.at[:, pl.ds(near * DH, (heads - near) * DH)], dk_far, sems.at[4])
+    far_copy.start()
     copies = []
 
     def store(src, dst, part):
-        at = pl.ds(part * wide, wide)
+        at = pl.ds(part * half * DH, half * DH)
         copies.append(pltpu.make_async_copy(src.at[:, at], dst.at[:, at], sems.at[len(copies)]))
         copies[-1].start()
 
@@ -265,10 +268,11 @@
             store(dv_ref, dv_hbm, head // half)
     for head in range(heads):
         at = columns(head)
-        if head == half:
-            v_copy.wait()
-        v = v_near[:, at] if head < half else v_far[:, columns(head - half)]
-        dk = dk_in[:, at] + dot(jnp.concatenate([v, v], 1), jnp.concatenate(states[head], 1), 1, 1)
+        if head == near:
+            far_copy.wait()
+        v = v_ref[:, at]
+        dk = dk_near[:, at] if head < near else dk_far[:, columns(head - near)]
+        dk = dk + dot(jnp.concatenate([v, v], 1), jnp.concatenate(states[head], 1), 1, 1)
         dk_ref[:, at] = (scale * dk).astype(dk_ref.dtype)
         if head % half == half - 1:
             store(dk_ref, dk_hbm, head // half)
@@ -287,6 +291,7 @@
     rows = wide // ctx
     per = 2 * tokens * DH * DH * heads
     all_tok = (tokens, wide)
+    near_tok = (tokens, wide - wide // 4)
     exchange = functools.partial(lax.all_to_all, axis_name="ctx", split_axis=0, concat_axis=0, tiled=True)
 
     inputs = [(a, "hbm") for a in (q, k, v, dy, gain)]
@@ -348,17 +353,17 @@
         return_kernel,
         "return_operands",
         [(k, "hbm"), (v, "hbm"), (dk_part, "hbm"), (dv_part, "hbm"), (gain_sum, ""), (gain_other, ""), (after, "hbm")],
-        [(all_tok, BF16, "vmem"), ((tokens, wide // 2), BF16, "vmem"), (all_tok, F32, "vmem"), (all_tok, F32, "vmem"), ((heads, DH), F32, "hbm")],
+        [(all_tok, BF16, "vmem"), (all_tok, BF16, "vmem"), (near_tok, F32, "vmem"), (all_tok, F32, "vmem"), ((heads, DH), F32, "hbm")],
         wide * DH,
         [pltpu.SemaphoreType.DMA((4,))],
     )
     d_key, d_value = call(
         functools.partial(last_kernel, scale),
         "key_value_gradients",
-        [(k_near, "vmem"), (v_near, "vmem"), (v, "hbm"), (suffix, ""), (dk_near, "vmem"), (dv_near, "vmem")],
+        [(k_near, "vmem"), (v_near, "vmem"), (suffix, ""), (dk_near, "vmem"), (dk_part, "hbm"), (dv_near, "vmem")],
         [(all_tok, BF16, "hbm raw"), (all_tok, BF16, "hbm raw")],
         4 * per,
-        [pltpu.VMEM((tokens, wide // 2), BF16)] + [pltpu.VMEM(all_tok, BF16)] * 2 + [pltpu.SemaphoreType.DMA((5,))],
+        [pltpu.VMEM((tokens, wide // 4), F32)] + [pltpu.VMEM(all_tok, BF16)] * 2 + [pltpu.SemaphoreType.DMA((5,))],
     )
     return (*(a[None] for a in (output, d_query, d_key, d_value)), grad_gain.reshape(wide))
 

time: 110 us -> 110 us (level)
    pallas_call x9, Pallas kernels: 20.1 us -> 21.2 us  [call(): pl.pallas_call(kernel, name=name, in_specs=[spec(w) for _, w in ins], out...]
where the time goes in v5:
time: 110 us
  blocking collectives  41.1 us (37%)
  waiting for transfers between devices  30.5 us (28%)
  Pallas kernels  21.2 us (19%)
  starting transfers between devices  16 us (15%)
    all_to_all x1, blocking collectives, body(): parts = exchange(local).reshape(ctx, rows, DH)  26.4 us
    pallas_call x9, Pallas kernels, call(): pl.pallas_call(kernel, name=name, in_specs=[spec(w) for _, w in ins], out...  21.2 us
    all_to_all x1, blocking collectives, body(): sums = lax.all_to_all(sums, 'heads', 0, 0, tiled=True)  14.7 us
    all_to_all x1, waiting for transfers between devices, body(): prefix = exchange(before.reshape(wide, DH))  13.5 us
    all_to_all x1, waiting for transfers between devices, body(): suffix = exchange(after.reshape(wide, DH))  7.95 us
    all_to_all x1, waiting for transfers between devices, body(): grad_parts = exchange(grad_local)  7.86 us
    all_to_all x1, starting transfers between devices, body(): grad_parts = exchange(grad_local)  4.81 us
    all_to_all x1, starting transfers between devices, body(): suffix = exchange(after.reshape(wide, DH))  4.68 us
  transfers between devices with their start and end apart: 4, of which 4 were waited for; matrix products, arithmetic and copies ran while one was open for 0% of the time, Pallas kernels for 9%

profile of v5, /device:TPU:64, one launch (start us, length us, event | category | flops | bytes accessed | tf_op | source)
XLA Modules:
  0.0 109.5 jit_solution(3013766073027562559)
XLA Ops:
  0.6 5.8 %key_value_states.1 = (f32[1024,128]{1,0:T(8,128)S(1)}, f32[256,1024]{1,0:T(8,128)S(1)}, bf16[256,1024]{1,0:T(8,128)(2,1)S(1)}, bf16[256,1024]{1,0:T(8,128)(2,1)S(1)}, f32[1,1024]{1,0:T(1,128)S(1)}) custom-call(bf16[256,1024]{1,0:T(8,128)(2,1)} %bitcast.25, bf16[256,1024]{1,0:T(8,128)(2,1)} %bitcast.17, bf16[256,1024]{1,0:T(8,128)(2,1)} %bitcast.21, ...), custom_call_target="tpu_custom_call" | custom-call | flops 268435456 | bytes 4726784 | tf_op jit(solution)/shard_map/key_value_states/pallas_call | solution.py:47
  6.4 26.4 %all_to_all.35.part_ref = f32[32,32,128]{2,1,0:T(8,128)S(1)} all-to-all(f32[32,32,128]{2,1,0:T(8,128)S(1)} %bitcast.16), channel_id=1, replica_groups=mesh['ctx'=32,'heads'=8,'dp'=2] {'ctx'}, dimensions={0} | all-to-all | bytes 1048576 | tf_op jit(solution)/shard_map/all_to_all | solution.py:301
  32.8 0.8 prefix.1
  33.7 4.6 %all-to-all-start.1 = ((f32[32,32,128]{2,1,0:T(8,128)}), f32[32,32,128]{2,1,0:T(8,128)S(1)}, u32[]{:S(2)}, u32[]{:S(2)}) async-start(f32[32,32,128]{2,1,0:T(8,128)} %prefix.1), calls=%async_computation.1 | async-start | bytes 1048576 | tf_op jit(solution)/shard_map/all_to_all | solution.py:315
  38.3 0.1 within_block.1
  38.4 13.5 %all-to-all-done.1 = f32[32,32,128]{2,1,0:T(8,128)S(1)} async-done(((f32[32,32,128]{2,1,0:T(8,128)}), f32[32,32,128]{2,1,0:T(8,128)S(1)}, u32[]{:S(2)}, u32[]{:S(2)}) %all-to-all-start.1) | async-done | bytes 524320 | tf_op jit(solution)/shard_map/all_to_all | solution.py:315
  51.9 0.6 attend.1
  52.5 0.0 copy-start
  52.5 14.7 %all_to_all.36.sums_ref = f32[8,4,128]{2,1,0:T(4,128)S(1)} all-to-all(f32[8,4,128]{2,1,0:T(4,128)S(1)} %get-tuple-element.41), channel_id=1, replica_groups=mesh['ctx'=32,'heads'=8,'dp'=2] {'heads'}, dimensions={0} | all-to-all | bytes 32768 | tf_op jit(solution)/shard_map/all_to_all | solution.py:323
  67.2 1.6 %grad_states.1 = (f32[32,40,128]{2,1,0:T(8,128)}, f32[2,256,128]{2,1,0:T(8,128)S(1)}) custom-call(f32[8,4,128]{2,1,0:T(4,128)S(1)} %all_to_all.36.sums_ref, bf16[256,1024]{1,0:T(8,128)(2,1)S(1)} %get-tuple-element.36.q_ref, f32[256,1024]{1,0:T(8,128)S(1)} %get-tuple-element.40.attn_ref, f32[1,1024]{1,0:T(1,128)S(1)} %get-tuple-element.35.gain_ref, ...), custom_call_target="tpu_custom_call" | custom-call | flops 134217728 | bytes 3035136 | tf_op jit(solution)/shard_map/grad_states/pallas_call | solution.py:47
  68.8 0.0 copy-done
  68.8 0.0 copy-start.1
  68.8 4.8 %all-to-all-start.3 = ((f32[32,40,128]{2,1,0:T(8,128)}), f32[32,40,128]{2,1,0:T(8,128)S(1)}, u32[]{:S(2)}, u32[]{:S(2)}) async-start(f32[32,40,128]{2,1,0:T(8,128)} %get-tuple-element.47), calls=%async_computation.3 | async-start | bytes 1310720 | tf_op jit(solution)/shard_map/all_to_all | solution.py:332
  73.6 0.0 copy-done.1
  73.6 7.1 %backward_within.1 = (bf16[256,1024]{1,0:T(8,128)(2,1)}, bf16[256,1024]{1,0:T(8,128)(2,1)}, f32[256,1024]{1,0:T(8,128)}, f32[256,1024]{1,0:T(8,128)}) custom-call(bf16[256,1024]{1,0:T(8,128)(2,1)} %bitcast.27, bf16[256,1024]{1,0:T(8,128)(2,1)} %bitcast.19, bf16[256,1024]{1,0:T(8,128)(2,1)} %bitcast.23, bf16[256,1024]{1,0:T(8,128)(2,1)} %bitcast.30, ...), custom_call_target="tpu_custom_call" | custom-call | flops 1476395008 | bytes 7081984 | tf_op jit(solution)/shard_map/backward_within/pallas_call | solution.py:47
  80.8 7.9 %all-to-all-done.3.part_ref = f32[32,40,128]{2,1,0:T(8,128)S(1)} async-done(((f32[32,40,128]{2,1,0:T(8,128)}), f32[32,40,128]{2,1,0:T(8,128)S(1)}, u32[]{:S(2)}, u32[]{:S(2)}) %all-to-all-start.3) | async-done | bytes 655392 | tf_op jit(solution)/shard_map/all_to_all | solution.py:332
  88.7 0.8 suffix.1
  89.5 4.7 %all-to-all-start.4 = ((f32[32,32,128]{2,1,0:T(8,128)}), f32[32,32,128]{2,1,0:T(8,128)S(1)}, u32[]{:S(2)}, u32[]{:S(2)}) async-start(f32[32,32,128]{2,1,0:T(8,128)} %get-tuple-element.49._), calls=%async_computation.4 | async-start | bytes 1048576 | tf_op jit(solution)/shard_map/all_to_all | solution.py:350
  94.2 1.9 %collective-permute-start = (f32[8,128]{1,0:T(8,128)S(1)}, f32[8,128]{1,0:T(8,128)S(1)}, u32[]{:S(2)}, u32[]{:S(2)}) collective-permute-start(f32[8,128]{1,0:T(8,128)S(1)} %get-tuple-element.48.gain_a), channel_id=1, source_target_pairs={{0,1},{1,0},{2,3},{3,2},{4,5},{5,4},{6,7},{7,6},{8,9},{9,8},{10,11... | collective-permute-start | bytes 12296 | tf_op jit(solution)/shard_map/ppermute | solution.py:351
  96.1 1.1 %collective-permute-done.gain_b = f32[8,128]{1,0:T(8,128)S(1)} collective-permute-done((f32[8,128]{1,0:T(8,128)S(1)}, f32[8,128]{1,0:T(8,128)S(1)}, u32[]{:S(2)}, u32[]{:S(2)}) %collective-permute-start) | collective-permute-done | bytes 4128 | tf_op jit(solution)/shard_map/ppermute | solution.py:351
  97.2 2.4 %return_operands.1 = (bf16[256,1024]{1,0:T(8,128)(2,1)S(1)}, bf16[256,1024]{1,0:T(8,128)(2,1)S(1)}, f32[256,768]{1,0:T(8,128)S(1)}, f32[256,1024]{1,0:T(8,128)S(1)}, f32[8,128]{1,0:T(8,128)}) custom-call(bf16[256,1024]{1,0:T(8,128)(2,1)} %bitcast.20, bf16[256,1024]{1,0:T(8,128)(2,1)} %bitcast.24, f32[256,1024]{1,0:T(8,128)} %get-tuple-element.45.dk_hbm.dk_part, ...), custom_call_target="tpu_custom_call" | custom-call | flops 131072 | bytes 6565888 | tf_op jit(solution)/shard_map/return_operands/pallas_call | solution.py:47
  99.6 8.0 %all-to-all-done.4 = f32[32,32,128]{2,1,0:T(8,128)S(1)} async-done(((f32[32,32,128]{2,1,0:T(8,128)}), f32[32,32,128]{2,1,0:T(8,128)S(1)}, u32[]{:S(2)}, u32[]{:S(2)}) %all-to-all-start.4) | async-done | bytes 524320 | tf_op jit(solution)/shard_map/all_to_all | solution.py:350
  107.6 1.9 %key_value_gradients.1 = (bf16[256,1024]{1,0:T(8,128)(2,1)}, bf16[256,1024]{1,0:T(8,128)(2,1)}) custom-call(bf16[256,1024]{1,0:T(8,128)(2,1)S(1)} %get-tuple-element.50.k_ref, bf16[256,1024]{1,0:T(8,128)(2,1)S(1)} %get-tuple-element.51.v_ref, f32[1024,128]{1,0:T(8,128)S(1)} %bitcast.15, f32[256,768]{1,0:T(8,128)S(1)} %get-tuple-element.52.dk_near, ...), custom_call_target="tpu_custom_call" | custom-call | flops 268435456 | bytes 5505024 | tf_op jit(solution)/shard_map/key_value_gradients/pallas_call | solution.py:47
Async XLA Ops:
  33.7 18.2 %all-to-all-start.1 = ((f32[32,32,128]{2,1,0:T(8,128)}), f32[32,32,128]{2,1,0:T(8,128)S(1)}, u32[]{:S(2)}, u32[]{:S(2)}) async-start(f32[32,32,128]{2,1,0:T(8,128)} %prefix.1), calls=%async_computation.1 | async-start | bytes 1048576 | tf_op jit(solution)/shard_map/all_to_all | solution.py:315
  52.5 16.3 %copy-start = (f32[256,1024]{1,0:T(8,128)}, f32[256,1024]{1,0:T(8,128)S(1)}, u32[]{:S(2)}) copy-start(f32[256,1024]{1,0:T(8,128)S(1)} %get-tuple-element.40.attn_ref) | copy-start | bytes 3145732
  68.8 4.8 %copy-start.1 = (f32[256,1024]{1,0:T(8,128)S(1)}, f32[256,1024]{1,0:T(8,128)}, u32[]{:S(2)}) copy-start(f32[256,1024]{1,0:T(8,128)} %copy-done) | copy-start | bytes 3145732
  68.8 19.8 %all-to-all-start.3 = ((f32[32,40,128]{2,1,0:T(8,128)}), f32[32,40,128]{2,1,0:T(8,128)S(1)}, u32[]{:S(2)}, u32[]{:S(2)}) async-start(f32[32,40,128]{2,1,0:T(8,128)} %get-tuple-element.47), calls=%async_computation.3 | async-start | bytes 1310720 | tf_op jit(solution)/shard_map/all_to_all | solution.py:332
  89.5 18.1 %all-to-all-start.4 = ((f32[32,32,128]{2,1,0:T(8,128)}), f32[32,32,128]{2,1,0:T(8,128)S(1)}, u32[]{:S(2)}, u32[]{:S(2)}) async-start(f32[32,32,128]{2,1,0:T(8,128)} %get-tuple-element.49._), calls=%async_computation.4 | async-start | bytes 1048576 | tf_op jit(solution)/shard_map/all_to_all | solution.py:350
  94.2 3.1 %collective-permute-start = (f32[8,128]{1,0:T(8,128)S(1)}, f32[8,128]{1,0:T(8,128)S(1)}, u32[]{:S(2)}, u32[]{:S(2)}) collective-permute-start(f32[8,128]{1,0:T(8,128)S(1)} %get-tuple-element.48.gain_a), channel_id=1, source_target_pairs={{0,1},{1,0},{2,3},{3,2},{4,5},{5,4},{6,7},{7,6},{8,9},{9,8},{10,11... | collective-permute-start | bytes 12296 | tf_op jit(solution)/shard_map/ppermute | solution.py:351

commit v6 on v5

--- a/solution.py
+++ b/solution.py
@@ -13,6 +13,8 @@
 F32 = jnp.float32
 BF16 = jnp.bfloat16
 VMEM_GRANT = 16 * 1024 * 1024
+FIRST = 7
+FIRST_HEADS = 4
 SUFFIX_OUT = "hbm"
 
 
@@ -110,12 +112,15 @@
     group = count // sems.shape[0]
     total = jnp.zeros(out_ref.shape[1:], F32)
     copies = []
+    left = [group] * sems.shape[0]
     for i in range(count):
-        place = count - 1 - i if reverse else i
+        place = ((count - 1 - i if reverse else i) - FIRST) % count
         out_ref[place] = total
         total = total + part_ref[place, :rows]
-        if i % group == group - 1:
-            at = pl.ds(place if reverse else place + 1 - group, group)
+        part = place // group
+        left[part] -= 1
+        if not left[part]:
+            at = pl.ds(part * group, group)
             copies.append(pltpu.make_async_copy(out_ref.at[at], out_hbm.at[at], sems.at[len(copies)]))
             copies[-1].start()
     return copies
@@ -201,7 +206,8 @@
         d_attn = (gain_ref[:, at] * dy_ref[:, at].astype(F32)) * inverse - attn_ref[:, at] * other
         upper, lower = halves(d_attn)
         q = q_ref[:, at]
-        state = dot(q, upper, 0, 0) + dot(q, lower, 0, 0)
+        both = dot(q, jnp.concatenate([upper, lower], 1), 0, 0)
+        state = both[:, :DH] + both[:, DH:]
         state_ref[head * per_head : (head + 1) * per_head, :rows, :] = state.reshape(per_head, rows, DH)
         if head % 2:
             send(pl.ds((head - 1) * per_head, 2 * per_head), pl.ds(0, rows))
@@ -292,7 +298,14 @@
     per = 2 * tokens * DH * DH * heads
     all_tok = (tokens, wide)
     near_tok = (tokens, wide - wide // 4)
-    exchange = functools.partial(lax.all_to_all, axis_name="ctx", split_axis=0, concat_axis=0, tiled=True)
+    exchange = functools.partial(
+        lax.all_to_all,
+        axis_name="ctx",
+        split_axis=0,
+        concat_axis=0,
+        tiled=True,
+        axis_index_groups=[[(FIRST + i) % ctx for i in range(ctx)]],
+    )
 
     inputs = [(a, "hbm") for a in (q, k, v, dy, gain)]
     near = [(all_tok, F32, "vmem"), (all_tok, BF16, "vmem"), (all_tok, BF16, "vmem"), ((1, wide), F32, "vmem")]
@@ -320,7 +333,14 @@
         [(all_tok, F32, "vmem"), ((shards, 2 * tokens // DH, DH), F32, "")],
         2 * per,
     )
-    sums = lax.all_to_all(sums, "heads", 0, 0, tiled=True)
+    sums = lax.all_to_all(
+        sums,
+        "heads",
+        0,
+        0,
+        tiled=True,
+        axis_index_groups=[[(FIRST_HEADS + i) % shards for i in range(shards)]],
+    )
     grad_local, factors = call(
         functools.partial(grad_state_kernel, width),
         "grad_states",

time: 110 us -> 105 us (0.955)
  the two profiles are of different devices: /device:TPU:64 before, /device:TPU:8 now
where the time goes in v6:
time: 105 us; the launch traced here: 104 us
  blocking collectives  35.7 us (34%)
  waiting for transfers between devices  24.9 us (24%)
  starting transfers between devices  21.5 us (20%)
  Pallas kernels  21.1 us (20%)
    all_to_all x1, blocking collectives, body(): parts = exchange(local).reshape(ctx, rows, DH)  25.2 us
    pallas_call x9, Pallas kernels, call(): pl.pallas_call(kernel, name=name, in_specs=[spec(w) for _, w in ins], out...  21.1 us
    all_to_all x1, waiting for transfers between devices, body(): prefix = exchange(before.reshape(wide, DH))  11.6 us
    all_to_all x1, blocking collectives, body(): lax.all_to_all(sums, 'heads', 0, 0, tiled=True, axis_index_groups=[[(FIRS...  10.5 us
    all_to_all x1, starting transfers between devices, body(): grad_parts = exchange(grad_local)  6.71 us
    all_to_all x1, starting transfers between devices, body(): suffix = exchange(after.reshape(wide, DH))  6.45 us
    all_to_all x1, starting transfers between devices, body(): prefix = exchange(before.reshape(wide, DH))  6.41 us
    all_to_all x1, waiting for transfers between devices, body(): suffix = exchange(after.reshape(wide, DH))  6.17 us
  transfers between devices with their start and end apart: 4, of which 4 were waited for; matrix products, arithmetic and copies ran while one was open for 0% of the time, Pallas kernels for 9%

profile of v6, /device:TPU:8, one launch (start us, length us, event | category | flops | bytes accessed | tf_op | source)
XLA Modules:
  0.0 104.0 jit_solution(2535287229759689121)
XLA Ops:
  0.6 5.8 %key_value_states.1 = (f32[1024,128]{1,0:T(8,128)S(1)}, f32[256,1024]{1,0:T(8,128)S(1)}, bf16[256,1024]{1,0:T(8,128)(2,1)S(1)}, bf16[256,1024]{1,0:T(8,128)(2,1)S(1)}, f32[1,1024]{1,0:T(1,128)S(1)}) custom-call(bf16[256,1024]{1,0:T(8,128)(2,1)} %bitcast.25, bf16[256,1024]{1,0:T(8,128)(2,1)} %bitcast.17, bf16[256,1024]{1,0:T(8,128)(2,1)} %bitcast.21, ...), custom_call_target="tpu_custom_call" | custom-call | flops 268435456 | bytes 4726784 | tf_op jit(solution)/shard_map/key_value_states/pallas_call | solution.py:49
  6.4 25.2 %all_to_all.35.part_ref = f32[32,32,128]{2,1,0:T(8,128)S(1)} all-to-all(f32[32,32,128]{2,1,0:T(8,128)S(1)} %bitcast.16), channel_id=1, replica_groups={{112,128,144,160,176,192,208,224,240,256,272,288,304,320,336,352,368,38..., dimensions={0} | all-to-all | bytes 1048576 | tf_op jit(solution)/shard_map/all_to_all | solution.py:314
  31.6 0.8 prefix.1
  32.4 6.4 %all-to-all-start.1 = ((f32[32,32,128]{2,1,0:T(8,128)}), f32[32,32,128]{2,1,0:T(8,128)S(1)}, u32[]{:S(2)}, u32[]{:S(2)}) async-start(f32[32,32,128]{2,1,0:T(8,128)} %prefix.1), calls=%async_computation.1 | async-start | bytes 1048576 | tf_op jit(solution)/shard_map/all_to_all | solution.py:328
  38.9 0.1 within_block.1
  38.9 11.6 %all-to-all-done.1 = f32[32,32,128]{2,1,0:T(8,128)S(1)} async-done(((f32[32,32,128]{2,1,0:T(8,128)}), f32[32,32,128]{2,1,0:T(8,128)S(1)}, u32[]{:S(2)}, u32[]{:S(2)}) %all-to-all-start.1) | async-done | bytes 524320 | tf_op jit(solution)/shard_map/all_to_all | solution.py:328
  50.5 0.6 attend.1
  51.1 0.0 copy-start
  51.1 10.5 %all_to_all.36.sums_ref = f32[8,4,128]{2,1,0:T(4,128)S(1)} all-to-all(f32[8,4,128]{2,1,0:T(4,128)S(1)} %get-tuple-element.41), channel_id=1, replica_groups={{8,10,12,14,0,2,4,6},{9,11,13,15,1,3,5,7},{24,26,28,30,16,18,20,22},{25..., dimensions={0} | all-to-all | bytes 32768 | tf_op jit(solution)/shard_map/all_to_all | solution.py:336
  61.7 1.5 %grad_states.1 = (f32[32,40,128]{2,1,0:T(8,128)}, f32[2,256,128]{2,1,0:T(8,128)S(1)}) custom-call(f32[8,4,128]{2,1,0:T(4,128)S(1)} %all_to_all.36.sums_ref, bf16[256,1024]{1,0:T(8,128)(2,1)S(1)} %get-tuple-element.36.q_ref, f32[256,1024]{1,0:T(8,128)S(1)} %get-tuple-element.40.attn_ref, f32[1,1024]{1,0:T(1,128)S(1)} %get-tuple-element.35.gain_ref, ...), custom_call_target="tpu_custom_call" | custom-call | flops 134217728 | bytes 3035136 | tf_op jit(solution)/shard_map/grad_states/pallas_call | solution.py:49
  63.2 0.0 copy-done
  63.2 0.0 copy-start.1
  63.2 6.7 %all-to-all-start.3 = ((f32[32,40,128]{2,1,0:T(8,128)}), f32[32,40,128]{2,1,0:T(8,128)S(1)}, u32[]{:S(2)}, u32[]{:S(2)}) async-start(f32[32,40,128]{2,1,0:T(8,128)} %get-tuple-element.47), calls=%async_computation.3 | async-start | bytes 1310720 | tf_op jit(solution)/shard_map/all_to_all | solution.py:352
  69.9 0.0 copy-done.1
  70.0 7.1 %backward_within.1 = (bf16[256,1024]{1,0:T(8,128)(2,1)}, bf16[256,1024]{1,0:T(8,128)(2,1)}, f32[256,1024]{1,0:T(8,128)}, f32[256,1024]{1,0:T(8,128)}) custom-call(bf16[256,1024]{1,0:T(8,128)(2,1)} %bitcast.27, bf16[256,1024]{1,0:T(8,128)(2,1)} %bitcast.19, bf16[256,1024]{1,0:T(8,128)(2,1)} %bitcast.23, bf16[256,1024]{1,0:T(8,128)(2,1)} %bitcast.30, ...), custom_call_target="tpu_custom_call" | custom-call | flops 1476395008 | bytes 7081984 | tf_op jit(solution)/shard_map/backward_within/pallas_call | solution.py:49
  77.1 6.0 %all-to-all-done.3.part_ref = f32[32,40,128]{2,1,0:T(8,128)S(1)} async-done(((f32[32,40,128]{2,1,0:T(8,128)}), f32[32,40,128]{2,1,0:T(8,128)S(1)}, u32[]{:S(2)}, u32[]{:S(2)}) %all-to-all-start.3) | async-done | bytes 655392 | tf_op jit(solution)/shard_map/all_to_all | solution.py:352
  83.1 0.8 suffix.1
  84.0 6.4 %all-to-all-start.4 = ((f32[32,32,128]{2,1,0:T(8,128)}), f32[32,32,128]{2,1,0:T(8,128)S(1)}, u32[]{:S(2)}, u32[]{:S(2)}) async-start(f32[32,32,128]{2,1,0:T(8,128)} %get-tuple-element.49._), calls=%async_computation.4 | async-start | bytes 1048576 | tf_op jit(solution)/shard_map/all_to_all | solution.py:370
  90.4 1.9 %collective-permute-start = (f32[8,128]{1,0:T(8,128)S(1)}, f32[8,128]{1,0:T(8,128)S(1)}, u32[]{:S(2)}, u32[]{:S(2)}) collective-permute-start(f32[8,128]{1,0:T(8,128)S(1)} %get-tuple-element.48.gain_a), channel_id=1, source_target_pairs={{0,1},{1,0},{2,3},{3,2},{4,5},{5,4},{6,7},{7,6},{8,9},{9,8},{10,11... | collective-permute-start | bytes 12296 | tf_op jit(solution)/shard_map/ppermute | solution.py:371
  92.3 1.1 %collective-permute-done.gain_b = f32[8,128]{1,0:T(8,128)S(1)} collective-permute-done((f32[8,128]{1,0:T(8,128)S(1)}, f32[8,128]{1,0:T(8,128)S(1)}, u32[]{:S(2)}, u32[]{:S(2)}) %collective-permute-start) | collective-permute-done | bytes 4128 | tf_op jit(solution)/shard_map/ppermute | solution.py:371
  93.5 2.4 %return_operands.1 = (bf16[256,1024]{1,0:T(8,128)(2,1)S(1)}, bf16[256,1024]{1,0:T(8,128)(2,1)S(1)}, f32[256,768]{1,0:T(8,128)S(1)}, f32[256,1024]{1,0:T(8,128)S(1)}, f32[8,128]{1,0:T(8,128)}) custom-call(bf16[256,1024]{1,0:T(8,128)(2,1)} %bitcast.20, bf16[256,1024]{1,0:T(8,128)(2,1)} %bitcast.24, f32[256,1024]{1,0:T(8,128)} %get-tuple-element.45.dk_hbm.dk_part, ...), custom_call_target="tpu_custom_call" | custom-call | flops 131072 | bytes 6565888 | tf_op jit(solution)/shard_map/return_operands/pallas_call | solution.py:49
  95.9 6.2 %all-to-all-done.4 = f32[32,32,128]{2,1,0:T(8,128)S(1)} async-done(((f32[32,32,128]{2,1,0:T(8,128)}), f32[32,32,128]{2,1,0:T(8,128)S(1)}, u32[]{:S(2)}, u32[]{:S(2)}) %all-to-all-start.4) | async-done | bytes 524320 | tf_op jit(solution)/shard_map/all_to_all | solution.py:370
  102.1 1.9 %key_value_gradients.1 = (bf16[256,1024]{1,0:T(8,128)(2,1)}, bf16[256,1024]{1,0:T(8,128)(2,1)}) custom-call(bf16[256,1024]{1,0:T(8,128)(2,1)S(1)} %get-tuple-element.50.k_ref, bf16[256,1024]{1,0:T(8,128)(2,1)S(1)} %get-tuple-element.51.v_ref, f32[1024,128]{1,0:T(8,128)S(1)} %bitcast.15, f32[256,768]{1,0:T(8,128)S(1)} %get-tuple-element.52.dk_near, ...), custom_call_target="tpu_custom_call" | custom-call | flops 268435456 | bytes 5505024 | tf_op jit(solution)/shard_map/key_value_gradients/pallas_call | solution.py:49
Async XLA Ops:
  32.4 18.1 %all-to-all-start.1 = ((f32[32,32,128]{2,1,0:T(8,128)}), f32[32,32,128]{2,1,0:T(8,128)S(1)}, u32[]{:S(2)}, u32[]{:S(2)}) async-start(f32[32,32,128]{2,1,0:T(8,128)} %prefix.1), calls=%async_computation.1 | async-start | bytes 1048576 | tf_op jit(solution)/shard_map/all_to_all | solution.py:328
  51.1 12.1 %copy-start = (f32[256,1024]{1,0:T(8,128)}, f32[256,1024]{1,0:T(8,128)S(1)}, u32[]{:S(2)}) copy-start(f32[256,1024]{1,0:T(8,128)S(1)} %get-tuple-element.40.attn_ref) | copy-start | bytes 3145732
  63.2 6.7 %copy-start.1 = (f32[256,1024]{1,0:T(8,128)S(1)}, f32[256,1024]{1,0:T(8,128)}, u32[]{:S(2)}) copy-start(f32[256,1024]{1,0:T(8,128)} %copy-done) | copy-start | bytes 3145732
  63.2 19.9 %all-to-all-start.3 = ((f32[32,40,128]{2,1,0:T(8,128)}), f32[32,40,128]{2,1,0:T(8,128)S(1)}, u32[]{:S(2)}, u32[]{:S(2)}) async-start(f32[32,40,128]{2,1,0:T(8,128)} %get-tuple-element.47), calls=%async_computation.3 | async-start | bytes 1310720 | tf_op jit(solution)/shard_map/all_to_all | solution.py:352
  84.0 18.1 %all-to-all-start.4 = ((f32[32,32,128]{2,1,0:T(8,128)}), f32[32,32,128]{2,1,0:T(8,128)S(1)}, u32[]{:S(2)}, u32[]{:S(2)}) async-start(f32[32,32,128]{2,1,0:T(8,128)} %get-tuple-element.49._), calls=%async_computation.4 | async-start | bytes 1048576 | tf_op jit(solution)/shard_map/all_to_all | solution.py:370
  90.4 3.1 %collective-permute-start = (f32[8,128]{1,0:T(8,128)S(1)}, f32[8,128]{1,0:T(8,128)S(1)}, u32[]{:S(2)}, u32[]{:S(2)}) collective-permute-start(f32[8,128]{1,0:T(8,128)S(1)} %get-tuple-element.48.gain_a), channel_id=1, source_target_pairs={{0,1},{1,0},{2,3},{3,2},{4,5},{5,4},{6,7},{7,6},{8,9},{9,8},{10,11... | collective-permute-start | bytes 12296 | tf_op jit(solution)/shard_map/ppermute | solution.py:371
